TPU v7x, 1024 devices: a whole 4x4x32 slice. The times are simulated.
1024 devices in a mesh: gx: 4 (over x), gy: 8 (over y, core), gz: 32 (over z).
Axes of the slice: x: 4, y: 4, z: 32, core: 2. Of those that a mesh axis runs over, the one named last changes fastest.
Arguments:
- thermal_level: float32 [256, 512, 512], P('gz', 'gy', 'gx'), may hold values from 0.3 to 2
- blend_fraction: float32 [256, 512, 512], P('gz', 'gy', 'gx'), may hold values from 0 to 1
- nonempty_blocks: int32 [256, 512, 4], P('gz', 'gy', 'gx'), may hold values 0 or 1
- appearance_weights: float32 [4, 7], replicated, may hold values from -4 to 4
- illumination_vector: float32 [3], replicated, may hold values from -4 to 4
Outputs:
- frame: float32 [4, 512, 512], P(None, ('gy', 'gz'), 'gx')
All inputs are finite; a program needn't handle non-finite values. No bound on the sum of `nonempty_blocks` on one device may be relied on, other than what follows from the above.
Results may differ from a plain program's by a relative error of at most 0.0003.
Values sent between devices are 32-bit elements; how exact they have to be, the bound alone decides.
No kernel may reach another device: no remote copies, remote signals or barrier semaphores. Data moves between devices by JAX's collectives and lax.ppermute only.
A program may use at most 32 MiB of HBM per device.

v0:
```python
import jax
import jax.numpy as jnp
from jax import lax
from jax.sharding import PartitionSpec as P


def padded_2(cells, sides, width):
    for axis, dim in sides:
        count = lax.axis_size(axis)
        ends = count - 1
        head = lax.slice_in_dim(cells, 0, width, axis=dim)
        tail = lax.slice_in_dim(cells, cells.shape[dim] - width, cells.shape[dim], axis=dim)
        cells = jnp.concatenate(
            [
                lax.ppermute(tail, axis, [(i, (i + 1) % count) for i in range(ends)]),
                cells,
                lax.ppermute(head, axis, [((i + 1) % count, i) for i in range(ends)]),
            ],
            axis=dim,
        )
    return cells


def partner(value, axis, stride):
    mask = 2**stride
    pairs = [(source, source ^ mask) for source in range(lax.axis_size(axis))]
    return lax.ppermute(value, axis, pairs)


def midpoint_difference(slab_field):
    centre = slab_field[1:-1, 1:-1, 1:-1]
    grad_z = (slab_field[2:, 1:-1, 1:-1] - slab_field[:-2, 1:-1, 1:-1]) * 0.5
    grad_y = (slab_field[1:-1, 2:, 1:-1] - slab_field[1:-1, :-2, 1:-1]) * 0.5
    grad_x = (slab_field[1:-1, 1:-1, 2:] - slab_field[1:-1, 1:-1, :-2]) * 0.5
    return (centre, grad_z, grad_y, grad_x)


def illuminate_samples(
    sheet_heat, sheet_blend, filled_flags, appearance_weights, illumination_vector, march_spacing
):
    heat_centred, heat_slope_forward, heat_slope_vertical, heat_slope_horizontal = (
        midpoint_difference(sheet_heat)
    )
    mix_c, mz_grad, my_grad, mx_grad = midpoint_difference(sheet_blend)
    temp_sq = (
        heat_slope_forward * heat_slope_forward
        + heat_slope_vertical * heat_slope_vertical
        + heat_slope_horizontal * heat_slope_horizontal
    )
    mix_sq = mz_grad * mz_grad + my_grad * my_grad + mx_grad * mx_grad
    lambert = (
        heat_slope_horizontal * illumination_vector[0]
        + heat_slope_vertical * illumination_vector[1]
        + heat_slope_forward * illumination_vector[2]
    ) / jnp.sqrt(temp_sq + 1.0)
    features = [
        heat_centred,
        mix_c,
        temp_sq / (1.0 + temp_sq),
        mix_sq / (1.0 + mix_sq),
        lambert,
        heat_centred * mix_c,
    ]
    linear = []
    for row_id in range(4):
        total = appearance_weights[row_id, 6] + jnp.zeros_like(heat_centred)
        for feat_id in range(6):
            total = total + appearance_weights[row_id, feat_id] * features[feat_id]
        linear.append(total)
    emitted_hues = jnp.stack(
        [jax.nn.sigmoid(linear[0]), jax.nn.sigmoid(linear[1]), jax.nn.sigmoid(linear[2])]
    )
    extinction = jax.nn.softplus(linear[3]) * filled_flags
    attenuated_share = 1.0 - jnp.exp(-march_spacing * extinction)
    return (attenuated_share, emitted_hues)


def brick_image(attenuated_share, emitted_hues):
    kept = 1.0 - attenuated_share
    transmit = jnp.concatenate([jnp.ones_like(kept[:1]), jnp.cumprod(kept, axis=0)[:-1]], axis=0)
    weights = attenuated_share * transmit
    colour_sum = jnp.sum(weights[None] * emitted_hues, axis=1)
    opacity = jnp.sum(weights, axis=0)
    return jnp.concatenate([colour_sum, opacity[None]], axis=0)


def clamp_edge(padded, position, dev_count, axis_dim):
    extent = padded.shape[axis_dim]
    lower = lax.slice_in_dim(padded, 0, 1, axis=axis_dim)
    first_row = lax.slice_in_dim(padded, 1, 2, axis=axis_dim)
    middle = lax.slice_in_dim(padded, 1, extent - 1, axis=axis_dim)
    last_row = lax.slice_in_dim(padded, extent - 2, extent - 1, axis=axis_dim)
    upper = lax.slice_in_dim(padded, extent - 1, extent, axis=axis_dim)
    lower = jnp.where(position == 0, first_row, lower)
    upper = jnp.where(position == dev_count - 1, last_row, upper)
    return jnp.concatenate([lower, middle, upper], axis=axis_dim)


def on_device(
    thermal_level, blend_fraction, nonempty_blocks, appearance_weights, illumination_vector
):
    sightline_samples, vertical_samples, lateral_samples = thermal_level.shape
    sampled_quantities = jnp.stack([thermal_level, blend_fraction])
    padded = padded_2(sampled_quantities, (("gx", 3), ("gy", 2), ("gz", 1)), 1)
    depth_count = lax.axis_size("gz")
    gz_index = lax.axis_index("gz")
    padded = clamp_edge(padded, gz_index, depth_count, 1)
    padded = clamp_edge(padded, lax.axis_index("gy"), lax.axis_size("gy"), 2)
    padded = clamp_edge(padded, lax.axis_index("gx"), lax.axis_size("gx"), 3)
    march_spacing = 2.0 / (sightline_samples * depth_count)
    filled_flags = jnp.repeat(nonempty_blocks, 128, axis=2).astype(jnp.float32)
    attenuated_share, emitted_hues = illuminate_samples(
        padded[0], padded[1], filled_flags, appearance_weights, illumination_vector, march_spacing
    )
    partial_image = brick_image(attenuated_share, emitted_hues)
    tile_rows = vertical_samples // depth_count
    current = partial_image.reshape(4, depth_count, tile_rows, lateral_samples)
    for bit_index in range(depth_count.bit_length() - 1):
        halves = current.shape[1] // 2
        paired = current.reshape(4, halves, 2, tile_rows, lateral_samples)
        my_bit = gz_index // 2**bit_index % 2
        retained = lax.dynamic_index_in_dim(paired, my_bit, axis=2, keepdims=False)
        outgoing = lax.dynamic_index_in_dim(paired, 1 - my_bit, axis=2, keepdims=False)
        received = partner(outgoing, "gz", bit_index)
        nearer = jnp.where(my_bit == 0, retained, received)
        farther = jnp.where(my_bit == 0, received, retained)
        current = nearer + (1.0 - nearer[3:4]) * farther
    composite = current.reshape(4, tile_rows, lateral_samples)
    return composite


def solution(mesh):
    placed = (P("gz", "gy", "gx"), P("gz", "gy", "gx"), P("gz", "gy", "gx"), P(), P())
    return jax.shard_map(
        on_device,
        mesh=mesh,
        in_specs=placed,
        out_specs=P(None, ("gy", "gz"), "gx"),
        check_vma=False,
    )
```

profile of v0, /device:TPU:24, one launch (start us, length us, event | category | flops | bytes accessed | tf_op | source)
XLA Modules:
  0.0 134.3 jit_solution(4265693217883161837)
XLA Ops:
  0.0 0.0 copy-start.1
  0.0 0.0 copy-start
  0.0 0.0 copy-start.3
  0.0 0.0 copy-start.4
  0.0 1.4 %slice_maximum_fusion = (f32[2,8,64,1]{3,2,1,0:T(8,128)S(1)}, f32[2,8,64,1]{3,2,1,0:T(8,128)S(1)}) fusion(f32[1,8,64,128]{3,2,1,0:T(8,128)} %bitcast.98, f32[1,8,64,128]{3,2,1,0:T(8,128)} %bitcast.103), kind=kLoop, calls=%fused_computation.11 | loop fusion | flops 2048 | bytes 532480 | tf_op jit(solution)/shard_map/stack | solution.py:103
  1.5 3.4 %collective-permute-start = (f32[2,8,64,1]{3,2,1,0:T(8,128)S(1)}, f32[2,8,64,1]{3,2,1,0:T(8,128)S(1)}, u32[]{:S(2)}, u32[]{:S(2)}) collective-permute-start(f32[2,8,64,1]{3,2,1,0:T(8,128)S(1)} %get-tuple-element.21), channel_id=1, source_target_pairs={{0,256},{256,512},{512,768},{1,257},{257,513},{513,769},{2,258},{2... | collective-permute-start | bytes 12296 | tf_op jit(solution)/shard_map/ppermute | solution.py:15
  4.9 0.0 copy-start.2
  4.9 1.3 collective-permute-start.1
  6.2 9.8 %collective-permute-done = f32[2,8,64,1]{3,2,1,0:T(8,128)S(1)} collective-permute-done((f32[2,8,64,1]{3,2,1,0:T(8,128)S(1)}, f32[2,8,64,1]{3,2,1,0:T(8,128)S(1)}, u32[]{:S(2)}, u32[]{:S(2)}) %collective-permute-start) | collective-permute-done | bytes 4128 | tf_op jit(solution)/shard_map/ppermute | solution.py:15
  16.0 4.2 %collective-permute-done.1 = f32[2,8,64,1]{3,2,1,0:T(8,128)S(1)} collective-permute-done((f32[2,8,64,1]{3,2,1,0:T(8,128)S(1)}, f32[2,8,64,1]{3,2,1,0:T(8,128)S(1)}, u32[]{:S(2)}, u32[]{:S(2)}) %collective-permute-start.1) | collective-permute-done | bytes 4128 | tf_op jit(solution)/shard_map/ppermute | solution.py:17
  20.2 0.0 copy-done.1
  20.2 0.0 copy-done
  20.2 0.2 pad_maximum_fusion.13
  20.4 1.9 %collective-permute-start.2 = (f32[2,8,1,130]{3,2,1,0:T(1,128)S(1)}, f32[2,8,1,130]{3,2,1,0:T(1,128)S(1)}, u32[]{:S(2)}, u32[]{:S(2)}) collective-permute-start(f32[2,8,1,130]{3,2,1,0:T(1,128)S(1)} %get-tuple-element.13), channel_id=1, source_target_pairs={{0,32},{32,64},{64,96},{96,128},{128,160},{160,192},{192,224},{1,3... | collective-permute-start | bytes 24968 | tf_op jit(solution)/shard_map/ppermute | solution.py:15
  22.3 3.6 %collective-permute-start.3 = (f32[2,8,1,130]{3,2,1,0:T(1,128)S(1)}, f32[2,8,1,130]{3,2,1,0:T(1,128)S(1)}, u32[]{:S(2)}, u32[]{:S(2)}) collective-permute-start(f32[2,8,1,130]{3,2,1,0:T(1,128)S(1)} %get-tuple-element.14), channel_id=1, source_target_pairs={{32,0},{64,32},{96,64},{128,96},{160,128},{192,160},{224,192},{33,... | collective-permute-start | bytes 24968 | tf_op jit(solution)/shard_map/ppermute | solution.py:17
  25.9 0.0 copy-done.3
  26.0 0.6 fusion.35
  28.5 0.0 copy-done.4
  28.5 0.0 collective-permute-done.2
  28.5 0.0 collective-permute-done.3
  28.5 0.1 pad_maximum_fusion.4
  28.7 3.8 %collective-permute-start.4 = (f32[2,1,66,130]{3,2,1,0:T(8,128)S(1)}, f32[2,1,66,130]{3,2,1,0:T(8,128)S(1)}, u32[]{:S(2)}, u32[]{:S(2)}) collective-permute-start(f32[2,1,66,130]{3,2,1,0:T(8,128)S(1)} %pad_maximum_fusion.4), channel_id=1, source_target_pairs={{0,1},{1,2},{2,3},{3,4},{4,5},{5,6},{6,7},{7,8},{8,9},{9,10},{10,1... | collective-permute-start | bytes 205928 | tf_op jit(solution)/shard_map/ppermute | solution.py:15
  32.5 0.0 copy-done.2
  32.5 0.7 fusion.33
  33.3 1.9 %collective-permute-done.4 = f32[2,1,66,130]{3,2,1,0:T(8,128)S(1)} collective-permute-done((f32[2,1,66,130]{3,2,1,0:T(8,128)S(1)}, f32[2,1,66,130]{3,2,1,0:T(8,128)S(1)}, u32[]{:S(2)}, u32[]{:S(2)}) %collective-permute-start.4) | collective-permute-done | bytes 68672 | tf_op jit(solution)/shard_map/ppermute | solution.py:15
  35.2 0.1 broadcast_select_fusion.1
  35.3 1.3 collective-permute-start.5
  36.6 0.7 fusion.34
  37.3 5.5 %collective-permute-done.5 = f32[2,1,66,130]{3,2,1,0:T(8,128)S(1)} collective-permute-done((f32[2,1,66,130]{3,2,1,0:T(8,128)S(1)}, f32[2,1,66,130]{3,2,1,0:T(8,128)S(1)}, u32[]{:S(2)}, u32[]{:S(2)}) %collective-permute-start.5) | collective-permute-done | bytes 68672 | tf_op jit(solution)/shard_map/ppermute | solution.py:17
  42.8 0.5 pad_maximum_fusion
  43.3 0.1 slice.282
  43.5 0.2 pad_maximum_fusion.1
  43.7 0.3 slice.287
  44.0 0.5 slice_select_fusion.1
  44.4 0.6 pad_maximum_fusion.2
  45.1 0.1 slice_bitcast_fusion.1
  45.2 5.2 %fusion.5 = (f32[8,64,128]{2,1,0:T(8,128)S(1)}, f32[8,64,128]{2,1,0:T(8,128)S(1)}, f32[8,64,128]{2,1,0:T(8,128)S(1)}, f32[8,64,128]{2,1,0:T(8,128)S(1)}) fusion(f32[10,66,130]{2,1,0:T(8,128)S(1)} %get-tuple-element.16, f32[10,66,130]{2,1,0:T(8,128)S(1)} %get-tuple-element.15, f32[8,64]{1,0:T(8,128)S(1)} %bitcast.120, f32[]{:T(128)} %bitcast.13, f32[]{:T(128)} %bitcast.9, ...), kind=kLoop, calls=%fused_computation.19 | loop fusion | flops 3538944 | bytes 4720680 | tf_op jit(solution)/shard_map/sub | solution.py:74
  50.5 4.6 %divide_bitcast_fusion.2 = f32[1,8,64,128]{3,2,1,0:T(8,128)S(1)} fusion(f32[8,64,128]{2,1,0:T(8,128)S(1)} %get-tuple-element.10, f32[8,64,128]{2,1,0:T(8,128)S(1)} %get-tuple-element.9, f32[8,64,128]{2,1,0:T(8,128)S(1)} %get-tuple-element.8, f32[10,66,130]{2,1,0:T(8,128)S(1)} %get-tuple-element.16, f32[10,66,130]{2,1,0:T(8,128)S(1)} %get-tuple-element.15, ...), kind=kLoop, calls=%fused_computation.36 | loop fusion | flops 1048576 | bytes 1572892 | tf_op jit(solution)/shard_map/stack | solution.py:70
  55.1 4.8 %divide_bitcast_fusion.1 = f32[1,8,64,128]{3,2,1,0:T(8,128)S(1)} fusion(f32[8,64,128]{2,1,0:T(8,128)S(1)} %get-tuple-element.10, f32[8,64,128]{2,1,0:T(8,128)S(1)} %get-tuple-element.9, f32[8,64,128]{2,1,0:T(8,128)S(1)} %get-tuple-element.8, f32[10,66,130]{2,1,0:T(8,128)S(1)} %get-tuple-element.16, f32[10,66,130]{2,1,0:T(8,128)S(1)} %get-tuple-element.15, ...), kind=kLoop, calls=%fused_computation.35 | loop fusion | flops 1048576 | bytes 1572892 | tf_op jit(solution)/shard_map/stack | solution.py:70
  59.9 4.7 %divide_bitcast_fusion = f32[1,8,64,128]{3,2,1,0:T(8,128)S(1)} fusion(f32[8,64,128]{2,1,0:T(8,128)S(1)} %get-tuple-element.10, f32[8,64,128]{2,1,0:T(8,128)S(1)} %get-tuple-element.9, f32[8,64,128]{2,1,0:T(8,128)S(1)} %get-tuple-element.8, f32[10,66,130]{2,1,0:T(8,128)S(1)} %get-tuple-element.16, f32[10,66,130]{2,1,0:T(8,128)S(1)} %get-tuple-element.15, ...), kind=kLoop, calls=%fused_computation.34 | loop fusion | flops 1048576 | bytes 1572892 | tf_op jit(solution)/shard_map/stack | solution.py:70
  64.6 0.1 fusion
  64.7 0.1 fusion.18
  64.8 3.9 %collective-permute-start.6 = (f32[4,16,2,128]{3,1,2,0:T(8,128)S(1)}, f32[4,16,2,128]{3,1,2,0:T(8,128)S(1)}, u32[]{:S(2)}, u32[]{:S(2)}) collective-permute-start(f32[4,16,2,128]{3,1,2,0:T(8,128)S(1)} %bitcast.117), channel_id=1, source_target_pairs={{0,1},{1,0},{2,3},{3,2},{4,5},{5,4},{6,7},{7,6},{8,9},{9,8},{10,11... | collective-permute-start | bytes 196616 | tf_op jit(solution)/shard_map/ppermute | solution.py:27
  68.7 2.2 %collective-permute-done.6 = f32[4,16,2,128]{3,1,2,0:T(8,128)S(1)} collective-permute-done((f32[4,16,2,128]{3,1,2,0:T(8,128)S(1)}, f32[4,16,2,128]{3,1,2,0:T(8,128)S(1)}, u32[]{:S(2)}, u32[]{:S(2)}) %collective-permute-start.6) | collective-permute-done | bytes 65568 | tf_op jit(solution)/shard_map/ppermute | solution.py:27
  71.0 0.1 constant_dynamic-slice_fusion.5
  71.0 7.5 %collective-permute-start.7 = (f32[4,8,2,128]{3,1,2,0:T(8,128)S(1)}, f32[4,8,2,128]{3,1,2,0:T(8,128)S(1)}, u32[]{:S(2)}, u32[]{:S(2)}) collective-permute-start(f32[4,8,2,128]{3,1,2,0:T(8,128)S(1)} %bitcast.118), channel_id=1, source_target_pairs={{0,2},{1,3},{2,0},{3,1},{4,6},{5,7},{6,4},{7,5},{8,10},{9,11},{10,... | collective-permute-start | bytes 98312 | tf_op jit(solution)/shard_map/ppermute | solution.py:27
  78.6 1.8 %collective-permute-done.7 = f32[4,8,2,128]{3,1,2,0:T(8,128)S(1)} collective-permute-done((f32[4,8,2,128]{3,1,2,0:T(8,128)S(1)}, f32[4,8,2,128]{3,1,2,0:T(8,128)S(1)}, u32[]{:S(2)}, u32[]{:S(2)}) %collective-permute-start.7) | collective-permute-done | bytes 32800 | tf_op jit(solution)/shard_map/ppermute | solution.py:27
  80.5 9.2 %collective-permute-start.8 = (f32[4,4,2,128]{3,2,1,0:T(2,128)S(1)}, f32[4,4,2,128]{3,2,1,0:T(2,128)S(1)}, u32[]{:S(2)}, u32[]{:S(2)}) collective-permute-start(f32[4,4,2,128]{3,2,1,0:T(2,128)S(1)} %bitcast.119), channel_id=1, source_target_pairs={{0,4},{1,5},{2,6},{3,7},{4,0},{5,1},{6,2},{7,3},{8,12},{9,13},{10,... | collective-permute-start | bytes 49160 | tf_op jit(solution)/shard_map/ppermute | solution.py:27
  89.8 1.7 %collective-permute-done.8 = f32[4,4,2,128]{3,2,1,0:T(2,128)S(1)} collective-permute-done((f32[4,4,2,128]{3,2,1,0:T(2,128)S(1)}, f32[4,4,2,128]{3,2,1,0:T(2,128)S(1)}, u32[]{:S(2)}, u32[]{:S(2)}) %collective-permute-start.8) | collective-permute-done | bytes 16416 | tf_op jit(solution)/shard_map/ppermute | solution.py:27
  91.5 15.7 %collective-permute-start.9 = (f32[4,2,2,128]{3,2,1,0:T(2,128)S(1)}, f32[4,2,2,128]{3,2,1,0:T(2,128)S(1)}, u32[]{:S(2)}, u32[]{:S(2)}) collective-permute-start(f32[4,2,2,128]{3,2,1,0:T(2,128)S(1)} %dynamic-slice_bitcast_fusion), channel_id=1, source_target_pairs={{0,8},{1,9},{2,10},{3,11},{4,12},{5,13},{6,14},{7,15},{8,0},{9,1},... | collective-permute-start | bytes 24584 | tf_op jit(solution)/shard_map/ppermute | solution.py:27
  107.3 1.6 %collective-permute-done.9 = f32[4,2,2,128]{3,2,1,0:T(2,128)S(1)} collective-permute-done((f32[4,2,2,128]{3,2,1,0:T(2,128)S(1)}, f32[4,2,2,128]{3,2,1,0:T(2,128)S(1)}, u32[]{:S(2)}, u32[]{:S(2)}) %collective-permute-start.9) | collective-permute-done | bytes 8224 | tf_op jit(solution)/shard_map/ppermute | solution.py:27
  108.9 23.2 %collective-permute-start.10 = (f32[4,1,2,128]{3,2,1,0:T(2,128)S(1)}, f32[4,1,2,128]{3,2,1,0:T(2,128)S(1)}, u32[]{:S(2)}, u32[]{:S(2)}) collective-permute-start(f32[4,1,2,128]{3,2,1,0:T(2,128)S(1)} %constant_dynamic-slice_fusion), channel_id=1, source_target_pairs={{0,16},{1,17},{2,18},{3,19},{4,20},{5,21},{6,22},{7,23},{8,24},{9,... | collective-permute-start | bytes 12296 | tf_op jit(solution)/shard_map/ppermute | solution.py:27
  132.1 1.6 %collective-permute-done.10 = f32[4,1,2,128]{3,2,1,0:T(2,128)S(1)} collective-permute-done((f32[4,1,2,128]{3,2,1,0:T(2,128)S(1)}, f32[4,1,2,128]{3,2,1,0:T(2,128)S(1)}, u32[]{:S(2)}, u32[]{:S(2)}) %collective-permute-start.10) | collective-permute-done | bytes 4128 | tf_op jit(solution)/shard_map/ppermute | solution.py:27
  133.7 0.6 add_bitcast_fusion
  (25 shorter events, 0.4 us)
Async XLA Ops:
  0.0 20.2 %copy-start.1 = (f32[8,64,128]{2,1,0:T(8,128)S(1)}, f32[8,64,128]{2,1,0:T(8,128)}, u32[]{:S(2)}) copy-start(f32[8,64,128]{2,1,0:T(8,128)} %param.5) | copy-start | bytes 786436
  0.0 20.2 %copy-start = (f32[8,64,128]{2,1,0:T(8,128)S(1)}, f32[8,64,128]{2,1,0:T(8,128)}, u32[]{:S(2)}) copy-start(f32[8,64,128]{2,1,0:T(8,128)} %param.6) | copy-start | bytes 786436
  0.0 25.9 %copy-start.3 = (f32[3]{0:T(128)S(1)}, f32[3]{0:T(128)}, u32[]{:S(2)}) copy-start(f32[3]{0:T(128)} %param.9) | copy-start | bytes 40
  0.0 28.5 %copy-start.4 = (s32[8,64,1]{1,2,0:T(1,128)S(1)}, s32[8,64,1]{1,2,0:T(1,128)}, u32[]{:S(2)}) copy-start(s32[8,64,1]{1,2,0:T(1,128)} %param.7) | copy-start | bytes 6148
  1.5 14.6 %collective-permute-start = (f32[2,8,64,1]{3,2,1,0:T(8,128)S(1)}, f32[2,8,64,1]{3,2,1,0:T(8,128)S(1)}, u32[]{:S(2)}, u32[]{:S(2)}) collective-permute-start(f32[2,8,64,1]{3,2,1,0:T(8,128)S(1)} %get-tuple-element.21), channel_id=1, source_target_pairs={{0,256},{256,512},{512,768},{1,257},{257,513},{513,769},{2,258},{2... | collective-permute-start | bytes 12296 | tf_op jit(solution)/shard_map/ppermute | solution.py:15
  4.9 27.6 %copy-start.2 = (f32[4,7]{1,0:T(4,128)S(1)}, f32[4,7]{1,0:T(4,128)}, u32[]{:S(2)}) copy-start(f32[4,7]{1,0:T(4,128)} %param.8) | copy-start | bytes 340
  4.9 15.3 %collective-permute-start.1 = (f32[2,8,64,1]{3,2,1,0:T(8,128)S(1)}, f32[2,8,64,1]{3,2,1,0:T(8,128)S(1)}, u32[]{:S(2)}, u32[]{:S(2)}) collective-permute-start(f32[2,8,64,1]{3,2,1,0:T(8,128)S(1)} %get-tuple-element.22), channel_id=1, source_target_pairs={{256,0},{512,256},{768,512},{257,1},{513,257},{769,513},{258,2},{5... | collective-permute-start | bytes 12296 | tf_op jit(solution)/shard_map/ppermute | solution.py:17
  20.4 8.2 %collective-permute-start.2 = (f32[2,8,1,130]{3,2,1,0:T(1,128)S(1)}, f32[2,8,1,130]{3,2,1,0:T(1,128)S(1)}, u32[]{:S(2)}, u32[]{:S(2)}) collective-permute-start(f32[2,8,1,130]{3,2,1,0:T(1,128)S(1)} %get-tuple-element.13), channel_id=1, source_target_pairs={{0,32},{32,64},{64,96},{96,128},{128,160},{160,192},{192,224},{1,3... | collective-permute-start | bytes 24968 | tf_op jit(solution)/shard_map/ppermute | solution.py:15
  22.3 6.2 %collective-permute-start.3 = (f32[2,8,1,130]{3,2,1,0:T(1,128)S(1)}, f32[2,8,1,130]{3,2,1,0:T(1,128)S(1)}, u32[]{:S(2)}, u32[]{:S(2)}) collective-permute-start(f32[2,8,1,130]{3,2,1,0:T(1,128)S(1)} %get-tuple-element.14), channel_id=1, source_target_pairs={{32,0},{64,32},{96,64},{128,96},{160,128},{192,160},{224,192},{33,... | collective-permute-start | bytes 24968 | tf_op jit(solution)/shard_map/ppermute | solution.py:17
  28.7 6.5 %collective-permute-start.4 = (f32[2,1,66,130]{3,2,1,0:T(8,128)S(1)}, f32[2,1,66,130]{3,2,1,0:T(8,128)S(1)}, u32[]{:S(2)}, u32[]{:S(2)}) collective-permute-start(f32[2,1,66,130]{3,2,1,0:T(8,128)S(1)} %pad_maximum_fusion.4), channel_id=1, source_target_pairs={{0,1},{1,2},{2,3},{3,4},{4,5},{5,6},{6,7},{7,8},{8,9},{9,10},{10,1... | collective-permute-start | bytes 205928 | tf_op jit(solution)/shard_map/ppermute | solution.py:15
  35.3 7.5 %collective-permute-start.5 = (f32[2,1,66,130]{3,2,1,0:T(8,128)S(1)}, f32[2,1,66,130]{3,2,1,0:T(8,128)S(1)}, u32[]{:S(2)}, u32[]{:S(2)}) collective-permute-start(f32[2,1,66,130]{3,2,1,0:T(8,128)S(1)} %get-tuple-element.12), channel_id=1, source_target_pairs={{1,0},{2,1},{3,2},{4,3},{5,4},{6,5},{7,6},{8,7},{9,8},{10,9},{11,1... | collective-permute-start | bytes 205928 | tf_op jit(solution)/shard_map/ppermute | solution.py:17
  64.8 6.2 %collective-permute-start.6 = (f32[4,16,2,128]{3,1,2,0:T(8,128)S(1)}, f32[4,16,2,128]{3,1,2,0:T(8,128)S(1)}, u32[]{:S(2)}, u32[]{:S(2)}) collective-permute-start(f32[4,16,2,128]{3,1,2,0:T(8,128)S(1)} %bitcast.117), channel_id=1, source_target_pairs={{0,1},{1,0},{2,3},{3,2},{4,5},{5,4},{6,7},{7,6},{8,9},{9,8},{10,11... | collective-permute-start | bytes 196616 | tf_op jit(solution)/shard_map/ppermute | solution.py:27
  71.0 9.4 %collective-permute-start.7 = (f32[4,8,2,128]{3,1,2,0:T(8,128)S(1)}, f32[4,8,2,128]{3,1,2,0:T(8,128)S(1)}, u32[]{:S(2)}, u32[]{:S(2)}) collective-permute-start(f32[4,8,2,128]{3,1,2,0:T(8,128)S(1)} %bitcast.118), channel_id=1, source_target_pairs={{0,2},{1,3},{2,0},{3,1},{4,6},{5,7},{6,4},{7,5},{8,10},{9,11},{10,... | collective-permute-start | bytes 98312 | tf_op jit(solution)/shard_map/ppermute | solution.py:27
  80.5 10.9 %collective-permute-start.8 = (f32[4,4,2,128]{3,2,1,0:T(2,128)S(1)}, f32[4,4,2,128]{3,2,1,0:T(2,128)S(1)}, u32[]{:S(2)}, u32[]{:S(2)}) collective-permute-start(f32[4,4,2,128]{3,2,1,0:T(2,128)S(1)} %bitcast.119), channel_id=1, source_target_pairs={{0,4},{1,5},{2,6},{3,7},{4,0},{5,1},{6,2},{7,3},{8,12},{9,13},{10,... | collective-permute-start | bytes 49160 | tf_op jit(solution)/shard_map/ppermute | solution.py:27
  91.5 17.3 %collective-permute-start.9 = (f32[4,2,2,128]{3,2,1,0:T(2,128)S(1)}, f32[4,2,2,128]{3,2,1,0:T(2,128)S(1)}, u32[]{:S(2)}, u32[]{:S(2)}) collective-permute-start(f32[4,2,2,128]{3,2,1,0:T(2,128)S(1)} %dynamic-slice_bitcast_fusion), channel_id=1, source_target_pairs={{0,8},{1,9},{2,10},{3,11},{4,12},{5,13},{6,14},{7,15},{8,0},{9,1},... | collective-permute-start | bytes 24584 | tf_op jit(solution)/shard_map/ppermute | solution.py:27
  108.9 24.8 %collective-permute-start.10 = (f32[4,1,2,128]{3,2,1,0:T(2,128)S(1)}, f32[4,1,2,128]{3,2,1,0:T(2,128)S(1)}, u32[]{:S(2)}, u32[]{:S(2)}) collective-permute-start(f32[4,1,2,128]{3,2,1,0:T(2,128)S(1)} %constant_dynamic-slice_fusion), channel_id=1, source_target_pairs={{0,16},{1,17},{2,18},{3,19},{4,20},{5,21},{6,22},{7,23},{8,24},{9,... | collective-permute-start | bytes 12296 | tf_op jit(solution)/shard_map/ppermute | solution.py:27
where the time goes:
time: 136 us; the launch traced here: 134 us
  starting transfers between devices  75 us (55%)
  waiting for transfers between devices  30.2 us (22%)
  other arithmetic  23.9 us (18%)
  local copies, waits for them, and re-layouts  2.7 us (2%)
  between operations  2.5 us (2%)
    ppermute x5, starting transfers between devices, partner(): return lax.ppermute(value, axis, pairs)  59.6 us
    another operation x3, other arithmetic, illuminate_samples(): jnp.stack([jax.nn.sigmoid(linear[0]), jax.nn.sigmoid(linear[1]), jax.nn.s...  14 us
    ppermute x3, waiting for transfers between devices, padded_2(): lax.ppermute(tail, axis, [(i, (i + 1) % count) for i in range(ends)])  11.7 us
    ppermute x3, waiting for transfers between devices, padded_2(): lax.ppermute(head, axis, [((i + 1) % count, i) for i in range(ends)])  9.67 us
    ppermute x3, starting transfers between devices, padded_2(): lax.ppermute(tail, axis, [(i, (i + 1) % count) for i in range(ends)])  9.18 us
    ppermute x5, waiting for transfers between devices, partner(): return lax.ppermute(value, axis, pairs)  8.81 us
    ppermute x3, starting transfers between devices, padded_2(): lax.ppermute(head, axis, [((i + 1) % count, i) for i in range(ends)])  6.23 us
    sub x1, other arithmetic, illuminate_samples(): attenuated_share = 1.0 - jnp.exp(-march_spacing * extinction)  5.24 us
  transfers between devices with their start and end apart: 11, of which 9 were waited for; matrix products, arithmetic and copies ran while one was open for 2% of the time, Pallas kernels for 0%

commit v1 on v0

v1 whole, which is shorter than its diff:
```python
import jax
import jax.numpy as jnp
from jax import lax
from jax.experimental import pallas as pl
from jax.experimental.pallas import tpu as pltpu
from jax.sharding import PartitionSpec as P

EXACT = lax.Precision.HIGHEST
F32 = jnp.float32


def face_kernel(heat, blend, x_lo, x_hi, y_lo, y_hi, z_lo, z_hi):
    deep, tall, wide = heat.shape
    row = lax.broadcasted_iota(jnp.int32, (8, wide), 0)
    lane = lax.broadcasted_iota(jnp.int32, (8, wide), 1)
    pick = (((row == 0) & (lane == 0)) | ((row == 1) & (lane == wide - 1))).astype(F32)
    for index, field in enumerate((heat, blend)):
        flat = field[...].reshape(deep * tall, wide)
        ends = lax.dot_general(
            pick, flat, (((1,), (1,)), ((), ())), precision=EXACT, preferred_element_type=F32
        )
        x_lo[index : index + 1, :] = ends[0:1]
        x_hi[index : index + 1, :] = ends[1:2]
        for z in range(deep):
            y_lo[index, z : z + 1, :] = field[z, 0:1, :]
            y_hi[index, z : z + 1, :] = field[z, tall - 1 : tall, :]
        z_lo[index] = field[0]
        z_hi[index] = field[deep - 1]


def faces(heat, blend):
    deep, tall, wide = heat.shape
    shapes = [(2, deep * tall)] * 2 + [(2, deep, wide)] * 2 + [(2, tall, wide)] * 2
    return pl.pallas_call(
        face_kernel, out_shape=[jax.ShapeDtypeStruct(s, F32) for s in shapes], name="faces"
    )(heat, blend)


def brick_kernel(
    spacing, order, place, weights, light, heat, blend, filled, x_lo, x_hi, y_lo, y_hi, z_lo, z_hi,
    x_own_lo, x_own_hi, image, x_step,
):
    deep, tall, wide = heat.shape
    at = [place[i] == 1 for i in range(6)]
    row8 = lax.broadcasted_iota(jnp.int32, (8, wide), 0)
    lane8 = lax.broadcasted_iota(jnp.int32, (8, wide), 1)
    spread = jnp.where((row8 < 2) & (lane8 == 0), -1.0, 0.0) + jnp.where(
        (row8 >= 2) & (row8 < 4) & (lane8 == wide - 1), 1.0, 0.0
    )
    below = jnp.where(at[0], x_own_lo[...], x_lo[...])
    above = jnp.where(at[1], x_own_hi[...], x_hi[...])
    for index in range(2):
        keep = (row8 % 2 == index).astype(F32)
        sides = jnp.concatenate([below, above, jnp.zeros((4, deep * tall), F32)], axis=0)
        x_step[index] = lax.dot_general(
            sides, spread * keep, (((0,), (0,)), ((), ())), precision=EXACT,
            preferred_element_type=F32,
        ).reshape(deep, tall, wide)
    w = [[weights[r, k] for k in range(7)] for r in range(4)]
    sun = [light[i] for i in range(3)]
    fields = (heat, blend)
    not_first = lane8 > 0
    not_last = lane8 < wide - 1
    for block in range(tall // 8):
        top = 8 * block
        rows = slice(top, top + 8)
        through = jnp.ones((8, wide), F32)
        sums = [jnp.zeros((8, wide), F32) for _ in range(4)]

        def cells(index, z):
            if z < 0:
                return jnp.where(at[4], fields[index][0, rows, :], z_lo[index, rows, :])
            if z == deep:
                return jnp.where(at[5], fields[index][deep - 1, rows, :], z_hi[index, rows, :])
            return fields[index][z, rows, :]

        for z in range(deep):
            slopes = []
            for index in range(2):
                field = fields[index]
                here = field[z, rows, :]
                dz = cells(index, z + 1) - cells(index, z - 1)
                if block == 0:
                    edge = jnp.where(at[2], field[z, 0:1, :], y_lo[index, z : z + 1, :])
                    up = jnp.concatenate([edge, field[z, 0:7, :]], axis=0)
                else:
                    up = field[z, top - 1 : top + 7, :]
                if top + 8 == tall:
                    edge = jnp.where(at[3], field[z, tall - 1 : tall, :], y_hi[index, z : z + 1, :])
                    down = jnp.concatenate([field[z, top + 1 : tall, :], edge], axis=0)
                else:
                    down = field[z, top + 1 : top + 9, :]
                dy = down - up
                right = jnp.where(not_last, pltpu.roll(here, wide - 1, 1), 0.0)
                left = jnp.where(not_first, pltpu.roll(here, 1, 1), 0.0)
                dx = right - left + x_step[index, z, rows, :]
                slopes.append((here, dz * 0.5, dy * 0.5, dx * 0.5))
            t, tz, ty, tx = slopes[0]
            m, mz, my, mx = slopes[1]
            t_sq = tz * tz + ty * ty + tx * tx
            m_sq = mz * mz + my * my + mx * mx
            inverse = lax.rsqrt(t_sq + 1.0)
            features = [
                t,
                m,
                t_sq * (inverse * inverse),
                m_sq / (1.0 + m_sq),
                (tx * sun[0] + ty * sun[1] + tz * sun[2]) * inverse,
                t * m,
            ]
            linear = []
            for r in range(4):
                total = w[r][6] + w[r][0] * features[0]
                for k in range(1, 6):
                    total = total + w[r][k] * features[k]
                linear.append(total)
            hues = [0.5 * jnp.tanh(0.5 * linear[r]) + 0.5 for r in range(3)]
            soft = jnp.maximum(linear[3], 0.0) + jnp.log1p(jnp.exp(-jnp.abs(linear[3])))
            occupied = filled[z, rows, :].astype(F32)
            absorbed = 1.0 - jnp.exp(soft * (occupied * -spacing))
            weight = absorbed * through
            through = through * (1.0 - absorbed)
            for r in range(3):
                sums[r] = sums[r] + weight * hues[r]
            sums[3] = sums[3] + weight
        for j in range(4):
            for r in range(4):
                image[order[4 * block + j], 2 * r : 2 * r + 2, :] = sums[r][2 * j : 2 * j + 2]


def over_kernel(order, parts, frame):
    wide = parts.shape[2]
    row = lax.broadcasted_iota(jnp.int32, (8, wide), 0)
    through = jnp.ones((8, wide), F32)
    total = jnp.zeros((8, wide), F32)
    for z in range(parts.shape[0]):
        part = parts[order[z]]
        veil = jnp.where(row >= 6, part, 0.0)
        veil = veil + pltpu.roll(veil, 4, 0)
        veil = veil + pltpu.roll(veil, 2, 0)
        total = total + through * part
        through = through * (1.0 - veil)
    for r in range(4):
        frame[r] = total[2 * r : 2 * r + 2]


def on_device(heat, blend, filled, weights, light):
    deep, tall, wide = heat.shape
    depth_count = lax.axis_size("gz")
    spacing = 2.0 / (deep * depth_count)
    own = faces(heat, blend)
    halos, place = [], []
    for axis, lo, hi in (("gx", own[0], own[1]), ("gy", own[2], own[3]), ("gz", own[4], own[5])):
        count = lax.axis_size(axis)
        halos.append(lax.ppermute(hi, axis, [(i, i + 1) for i in range(count - 1)]))
        halos.append(lax.ppermute(lo, axis, [(i + 1, i) for i in range(count - 1)]))
        place += [lax.axis_index(axis) == 0, lax.axis_index(axis) == count - 1]
    place = jnp.stack(place).astype(jnp.int32)
    first = depth_count // 2
    group = [(first + i) % depth_count for i in range(depth_count)]
    order = [group.index(z) for z in range(depth_count)]
    smem = pl.BlockSpec(memory_space=pltpu.SMEM)
    vmem = pl.BlockSpec(memory_space=pltpu.VMEM)

    def brick(*refs):
        brick_kernel(spacing, order, *refs)

    def over(*refs):
        over_kernel(order, *refs)

    image = pl.pallas_call(
        brick,
        out_shape=jax.ShapeDtypeStruct((depth_count, 8, wide), F32),
        in_specs=[smem] * 3 + [vmem] * 11,
        scratch_shapes=[pltpu.VMEM((2, deep, tall, wide), F32)],
        name="brick",
    )(place, weights, light, heat, blend, filled, *halos, own[0], own[1])
    parts = lax.all_to_all(image, "gz", 0, 0, tiled=True, axis_index_groups=[group])
    return pl.pallas_call(
        over, out_shape=jax.ShapeDtypeStruct((4, tall // depth_count, wide), F32), name="over"
    )(parts)


def solution(mesh):
    placed = (P("gz", "gy", "gx"), P("gz", "gy", "gx"), P("gz", "gy", "gx"), P(), P())
    return jax.shard_map(
        on_device,
        mesh=mesh,
        in_specs=placed,
        out_specs=P(None, ("gy", "gz"), "gx"),
        check_vma=False,
    )
```

time: 136 us -> 76.4 us (0.56)
  the two profiles are of different devices: /device:TPU:24 before, /device:TPU:1 now
where the time goes in v1:
time: 76.4 us; the launch traced here: 75.9 us
  blocking collectives  41.6 us (54%)
  starting transfers between devices  22.5 us (29%)
  Pallas kernels  7.26 us (10%)
  local copies, waits for them, and re-layouts  2.2 us (3%)
  waiting for transfers between devices  1.63 us (2%)
    all_to_all x1, blocking collectives, on_device(): lax.all_to_all(image, 'gz', 0, 0, tiled=True, axis_index_groups=[group])  41.6 us
    ppermute x3, starting transfers between devices, on_device(): halos.append(lax.ppermute(hi, axis, [(i, i + 1) for i in range(count - 1)]))  11.8 us
    ppermute x3, starting transfers between devices, on_device(): halos.append(lax.ppermute(lo, axis, [(i + 1, i) for i in range(count - 1)]))  10.7 us
    pallas_call x1, Pallas kernels, on_device(): pl.pallas_call(brick, out_shape=jax.ShapeDtypeStruct((depth_count, 8, wid...  3.56 us
    pallas_call x1, Pallas kernels, faces(): pl.pallas_call(face_kernel, out_shape=[jax.ShapeDtypeStruct(s, F32) for s...  2.16 us
    unnamed x19, local copies, waits for them, and re-layouts  2.1 us
    ppermute x3, waiting for transfers between devices, on_device(): halos.append(lax.ppermute(lo, axis, [(i + 1, i) for i in range(count - 1)]))  1.62 us
    pallas_call x1, Pallas kernels, on_device(): pl.pallas_call(over, out_shape=jax.ShapeDtypeStruct((4, tall // depth_cou...  1.54 us
  transfers between devices with their start and end apart: 6, of which 1 were waited for; matrix products, arithmetic and copies ran while one was open for 2% of the time, Pallas kernels for 0%

profile of v1, /device:TPU:1, one launch (start us, length us, event | category | flops | bytes accessed | tf_op | source)
XLA Modules:
  0.0 75.9 jit_solution(14865638683455090439)
XLA Ops:
  0.0 2.2 %faces.1 = (f32[2,512]{1,0:T(2,128)}, f32[2,512]{1,0:T(2,128)}, f32[2,8,128]{2,1,0:T(8,128)}, f32[2,8,128]{2,1,0:T(8,128)}, f32[2,64,128]{2,1,0:T(8,128)}, /*index=5*/f32[2,64,128]{2,1,0:T(8,128)}) custom-call(f32[8,64,128]{2,1,0:T(8,128)} %refs_3_.1, f32[8,64,128]{2,1,0:T(8,128)} %refs_4_.1), custom_call_target="tpu_custom_call" | custom-call | tf_op jit(solution)/shard_map/faces/pallas_call | solution.py:34
  2.2 0.0 copy-start.6
  2.2 4.4 %collective-permute-start.4 = (f32[2,64,128]{2,1,0:T(8,128)}, f32[2,64,128]{2,1,0:T(8,128)S(1)}, u32[]{:S(2)}, u32[]{:S(2)}) collective-permute-start(f32[2,64,128]{2,1,0:T(8,128)} %get-tuple-element.15), channel_id=1, source_target_pairs={{0,1},{1,2},{2,3},{3,4},{4,5},{5,6},{6,7},{7,8},{8,9},{9,10},{10,1... | collective-permute-start | bytes 196616 | tf_op jit(solution)/shard_map/ppermute | solution.py:155
  6.5 0.0 copy-start.5
  6.6 1.3 %collective-permute-start.5 = (f32[2,64,128]{2,1,0:T(8,128)}, f32[2,64,128]{2,1,0:T(8,128)S(1)}, u32[]{:S(2)}, u32[]{:S(2)}) collective-permute-start(f32[2,64,128]{2,1,0:T(8,128)} %get-tuple-element.16), channel_id=1, source_target_pairs={{1,0},{2,1},{3,2},{4,3},{5,4},{6,5},{7,6},{8,7},{9,8},{10,9},{11,1... | collective-permute-start | bytes 196616 | tf_op jit(solution)/shard_map/ppermute | solution.py:156
  7.9 0.0 copy-done.6
  7.9 3.1 %collective-permute-start = (f32[2,512]{1,0:T(2,128)S(1)}, f32[2,512]{1,0:T(2,128)S(1)}, u32[]{:S(2)}, u32[]{:S(2)}) collective-permute-start(f32[2,512]{1,0:T(2,128)S(1)} %copy-done.6), channel_id=1, source_target_pairs={{0,256},{256,512},{512,768},{1,257},{257,513},{513,769},{2,258},{2... | collective-permute-start | bytes 12296 | tf_op jit(solution)/shard_map/ppermute | solution.py:155
  11.0 4.3 %collective-permute-start.2 = (f32[2,8,128]{2,1,0:T(8,128)}, f32[2,8,128]{2,1,0:T(8,128)S(1)}, u32[]{:S(2)}, u32[]{:S(2)}) collective-permute-start(f32[2,8,128]{2,1,0:T(8,128)} %get-tuple-element.13), channel_id=1, source_target_pairs={{0,32},{32,64},{64,96},{96,128},{128,160},{160,192},{192,224},{1,3... | collective-permute-start | bytes 24584 | tf_op jit(solution)/shard_map/ppermute | solution.py:155
  15.3 8.1 %collective-permute-start.3 = (f32[2,8,128]{2,1,0:T(8,128)}, f32[2,8,128]{2,1,0:T(8,128)S(1)}, u32[]{:S(2)}, u32[]{:S(2)}) collective-permute-start(f32[2,8,128]{2,1,0:T(8,128)} %get-tuple-element.14), channel_id=1, source_target_pairs={{32,0},{64,32},{96,64},{128,96},{160,128},{192,160},{224,192},{33,... | collective-permute-start | bytes 24584 | tf_op jit(solution)/shard_map/ppermute | solution.py:156
  23.4 0.0 collective-permute-done.refs_6_
  23.5 0.0 copy-start.7
  23.5 0.0 copy-done.5
  23.5 1.3 %collective-permute-start.1 = (f32[2,512]{1,0:T(2,128)S(1)}, f32[2,512]{1,0:T(2,128)S(1)}, u32[]{:S(2)}, u32[]{:S(2)}) collective-permute-start(f32[2,512]{1,0:T(2,128)S(1)} %copy-done.5), channel_id=1, source_target_pairs={{256,0},{512,256},{768,512},{257,1},{513,257},{769,513},{258,2},{5... | collective-permute-start | bytes 12296 | tf_op jit(solution)/shard_map/ppermute | solution.py:156
  24.8 0.0 copy-done.7
  24.8 0.0 copy-start.4
  24.8 0.1 stack.27
  24.9 0.6 convert_element_type.3.refs_0_
  25.5 0.0 copy-done.4
  25.5 0.9 %copy.6.refs_5_ = s32[8,64,1]{2,1,0:T(8,128)} copy(s32[8,64,1]{1,2,0:T(1,128)S(1)} %copy-done.4) | data formatting | bytes 4096 | tf_op args[2]
  26.4 1.6 %collective-permute-done.1.refs_7_ = f32[2,512]{1,0:T(2,128)S(1)} collective-permute-done((f32[2,512]{1,0:T(2,128)S(1)}, f32[2,512]{1,0:T(2,128)S(1)}, u32[]{:S(2)}, u32[]{:S(2)}) %collective-permute-start.1) | collective-permute-done | bytes 4128 | tf_op jit(solution)/shard_map/ppermute | solution.py:156
  28.0 0.0 copy-start.8
  28.0 0.0 collective-permute-done.2.refs_8_
  28.0 0.0 copy-start.2
  28.0 0.0 collective-permute-done.3.refs_9_
  28.0 0.0 copy-start.3
  28.0 0.0 collective-permute-done.4.refs_10_
  28.0 0.0 copy-start
  28.0 0.0 collective-permute-done.5.refs_11_
  28.0 0.5 copy-done.8
  28.6 0.0 copy-done.2
  28.6 0.0 copy-done.3
  28.6 0.0 copy-done
  28.6 0.0 copy-start.1
  28.6 0.6 copy-done.1
  29.2 3.6 %brick.1 = f32[32,8,128]{2,1,0:T(8,128)} custom-call(s32[6]{0:T(128)} %convert_element_type.3.refs_0_, f32[4,7]{1,0:T(4,128)} %refs_1_.1, f32[3]{0:T(128)} %refs_2_.1, f32[8,64,128]{2,1,0:T(8,128)} %refs_3_.1, f32[8,64,128]{2,1,0:T(8,128)} %refs_4_.1, s32[8,64,1]{2,1,0:T(8,128)} %copy.6.refs_5_, f32[2,512]{1,0:T(2,128)} %copy-done.7, f32[2,512]{1,0:T(2,128)} %copy-done.8, ...), custom_call_target="tpu_custom_call" | custom-call | tf_op jit(solution)/shard_map/brick/pallas_call | solution.py:171
  32.8 41.6 %all_to_all.5.refs_0_ = f32[32,8,128]{2,1,0:T(8,128)} all-to-all(f32[32,8,128]{2,1,0:T(8,128)} %brick.1), channel_id=1, replica_groups={{16,17,18,19,20,21,22,23,24,25,26,27,28,29,30,31,0,1,2,3,4,5,6,7,8,9,10..., dimensions={0} | all-to-all | bytes 262144 | tf_op jit(solution)/shard_map/all_to_all | solution.py:178
  74.4 1.5 %over.1 = f32[4,2,128]{2,1,0:T(2,128)} custom-call(f32[32,8,128]{2,1,0:T(8,128)} %all_to_all.5.refs_0_), custom_call_target="tpu_custom_call" | custom-call | tf_op jit(solution)/shard_map/over/pallas_call | solution.py:179
Async XLA Ops:
  2.2 5.7 %copy-start.6 = (f32[2,512]{1,0:T(2,128)S(1)}, f32[2,512]{1,0:T(2,128)}, u32[]{:S(2)}) copy-start(f32[2,512]{1,0:T(2,128)} %get-tuple-element.11.refs_13_) | copy-start | bytes 12292
  2.2 25.8 %collective-permute-start.4 = (f32[2,64,128]{2,1,0:T(8,128)}, f32[2,64,128]{2,1,0:T(8,128)S(1)}, u32[]{:S(2)}, u32[]{:S(2)}) collective-permute-start(f32[2,64,128]{2,1,0:T(8,128)} %get-tuple-element.15), channel_id=1, source_target_pairs={{0,1},{1,2},{2,3},{3,4},{4,5},{5,6},{6,7},{7,8},{8,9},{9,10},{10,1... | collective-permute-start | bytes 196616 | tf_op jit(solution)/shard_map/ppermute | solution.py:155
  6.5 16.9 %copy-start.5 = (f32[2,512]{1,0:T(2,128)S(1)}, f32[2,512]{1,0:T(2,128)}, u32[]{:S(2)}) copy-start(f32[2,512]{1,0:T(2,128)} %get-tuple-element.12.refs_12_) | copy-start | bytes 12292
  6.6 21.5 %collective-permute-start.5 = (f32[2,64,128]{2,1,0:T(8,128)}, f32[2,64,128]{2,1,0:T(8,128)S(1)}, u32[]{:S(2)}, u32[]{:S(2)}) collective-permute-start(f32[2,64,128]{2,1,0:T(8,128)} %get-tuple-element.16), channel_id=1, source_target_pairs={{1,0},{2,1},{3,2},{4,3},{5,4},{6,5},{7,6},{8,7},{9,8},{10,9},{11,1... | collective-permute-start | bytes 196616 | tf_op jit(solution)/shard_map/ppermute | solution.py:156
  7.9 15.6 %collective-permute-start = (f32[2,512]{1,0:T(2,128)S(1)}, f32[2,512]{1,0:T(2,128)S(1)}, u32[]{:S(2)}, u32[]{:S(2)}) collective-permute-start(f32[2,512]{1,0:T(2,128)S(1)} %copy-done.6), channel_id=1, source_target_pairs={{0,256},{256,512},{512,768},{1,257},{257,513},{513,769},{2,258},{2... | collective-permute-start | bytes 12296 | tf_op jit(solution)/shard_map/ppermute | solution.py:155
  11.0 17.0 %collective-permute-start.2 = (f32[2,8,128]{2,1,0:T(8,128)}, f32[2,8,128]{2,1,0:T(8,128)S(1)}, u32[]{:S(2)}, u32[]{:S(2)}) collective-permute-start(f32[2,8,128]{2,1,0:T(8,128)} %get-tuple-element.13), channel_id=1, source_target_pairs={{0,32},{32,64},{64,96},{96,128},{128,160},{160,192},{192,224},{1,3... | collective-permute-start | bytes 24584 | tf_op jit(solution)/shard_map/ppermute | solution.py:155
  15.3 12.7 %collective-permute-start.3 = (f32[2,8,128]{2,1,0:T(8,128)}, f32[2,8,128]{2,1,0:T(8,128)S(1)}, u32[]{:S(2)}, u32[]{:S(2)}) collective-permute-start(f32[2,8,128]{2,1,0:T(8,128)} %get-tuple-element.14), channel_id=1, source_target_pairs={{32,0},{64,32},{96,64},{128,96},{160,128},{192,160},{224,192},{33,... | collective-permute-start | bytes 24584 | tf_op jit(solution)/shard_map/ppermute | solution.py:156
  23.5 1.3 %copy-start.7 = (f32[2,512]{1,0:T(2,128)}, f32[2,512]{1,0:T(2,128)S(1)}, u32[]{:S(2)}) copy-start(f32[2,512]{1,0:T(2,128)S(1)} %collective-permute-done.refs_6_) | copy-start | bytes 12292
  23.5 4.5 %collective-permute-start.1 = (f32[2,512]{1,0:T(2,128)S(1)}, f32[2,512]{1,0:T(2,128)S(1)}, u32[]{:S(2)}, u32[]{:S(2)}) collective-permute-start(f32[2,512]{1,0:T(2,128)S(1)} %copy-done.5), channel_id=1, source_target_pairs={{256,0},{512,256},{768,512},{257,1},{513,257},{769,513},{258,2},{5... | collective-permute-start | bytes 12296 | tf_op jit(solution)/shard_map/ppermute | solution.py:156
  24.8 0.7 copy-start.4
  28.0 0.6 copy-start.8
  28.0 0.6 copy-start.2
  28.0 0.6 copy-start.3
  28.0 0.6 copy-start
  28.6 0.6 copy-start.1

commit v2 on v1

v2 whole, which is shorter than its diff:
```python
import jax
import jax.numpy as jnp
from jax import lax
from jax.experimental import pallas as pl
from jax.experimental.pallas import tpu as pltpu
from jax.sharding import PartitionSpec as P

F32 = jnp.float32
SMALL = pltpu.CompilerParams(vmem_limit_bytes=8 * 2**20)


def face_kernel(heat, blend, x_lo, x_hi, y_lo, y_hi, z_lo, z_hi):
    deep, tall, wide = heat.shape
    for index, field in enumerate((heat, blend)):
        z_lo[index] = field[0]
        z_hi[index] = field[deep - 1]
        y_lo[index] = jnp.concatenate([field[z, 0:1, :] for z in range(deep)], axis=0)
        y_hi[index] = jnp.concatenate([field[z, tall - 1 : tall, :] for z in range(deep)], axis=0)
    lane = lax.broadcasted_iota(jnp.int32, (wide, wide), 1)
    slabs = wide // tall
    for part in range(deep * tall // wide):
        t = heat[slabs * part : slabs * (part + 1)].reshape(wide, wide)
        m = blend[slabs * part : slabs * (part + 1)].reshape(wide, wide)
        ends = jnp.where(lane == 0, t, pltpu.roll(t, 2, 1))
        more = jnp.where(lane == 2, pltpu.roll(m, 2, 1), pltpu.roll(m, 4, 1))
        turned = jnp.where(lane < 2, ends, more).T
        here = slice(wide * part, wide * (part + 1))
        x_lo[0:1, here] = turned[0:1]
        x_hi[0:1, here] = turned[1:2]
        x_lo[1:2, here] = turned[2:3]
        x_hi[1:2, here] = turned[3:4]


def faces(heat, blend):
    deep, tall, wide = heat.shape
    shapes = [(2, deep * tall)] * 2 + [(2, deep, wide)] * 2 + [(2, tall, wide)] * 2
    return pl.pallas_call(
        face_kernel,
        out_shape=[jax.ShapeDtypeStruct(s, F32) for s in shapes],
        compiler_params=SMALL,
        name="faces",
    )(heat, blend)


def split3(values):
    high = values.astype(jnp.bfloat16).astype(F32)
    rest = values - high
    middle = rest.astype(jnp.bfloat16).astype(F32)
    return [high, middle, rest - middle]


def brick_kernel(
    spacing, order, weights, light, heat, blend, filled, x_lo, x_hi, y_lo, y_hi, z_lo, z_hi,
    x_own_lo, x_own_hi, image, x_step, veil,
):
    deep, tall, wide = heat.shape
    at = []
    for axis in ("gx", "gy", "gz"):
        at += [lax.axis_index(axis) == 0, lax.axis_index(axis) == lax.axis_size(axis) - 1]
    below = jnp.where(at[0], x_own_lo[...], x_lo[...])
    above = jnp.where(at[1], x_own_hi[...], x_hi[...])
    sides = jnp.concatenate([below, above, jnp.zeros((4, deep * tall), F32)], axis=0)
    sides = jnp.concatenate(split3(sides) + [jnp.zeros_like(sides)], axis=0).astype(jnp.bfloat16)
    row = lax.broadcasted_iota(jnp.int32, (32, 2 * wide), 0)
    side = row % 8
    column = lax.broadcasted_iota(jnp.int32, (32, 2 * wide), 1)
    spread = jnp.where(
        (side < 2) & (column == side * wide), -1.0,
        jnp.where((side >= 2) & (side < 4) & (column == (side - 2) * wide + wide - 1), 1.0, 0.0),
    ).astype(jnp.bfloat16)
    across = (((0,), (0,)), ((), ()))
    x_step[...] = lax.dot_general(sides, spread, across, preferred_element_type=F32)
    slab = lax.broadcasted_iota(jnp.int32, (deep, deep * wide), 0)
    column = lax.broadcasted_iota(jnp.int32, (deep, deep * wide), 1)
    same = (column // wide == slab).astype(F32)
    veil[...] = lax.dot_general(
        filled[...].astype(F32), same, across, preferred_element_type=F32
    ) * (-spacing)
    half = [0.5, 0.5, 0.5, 1.0]
    w = [[weights[r, k] * half[r] for k in range(7)] for r in range(4)]
    base = [w[r][6] + w[r][2] + w[r][3] for r in range(4)]
    sun = [light[i] * 0.5 for i in range(3)]
    fields = (heat, blend)
    lane8 = lax.broadcasted_iota(jnp.int32, (8, wide), 1)
    not_first = lane8 > 0
    not_last = lane8 < wide - 1
    for block in range(tall // 8):
        top = 8 * block
        rows = slice(top, top + 8)
        through = jnp.ones((8, wide), F32)
        sums = [jnp.zeros((8, wide), F32) for _ in range(4)]

        def cells(index, z):
            if z < 0:
                return jnp.where(at[4], fields[index][0, rows, :], z_lo[index, rows, :])
            if z == deep:
                return jnp.where(at[5], fields[index][deep - 1, rows, :], z_hi[index, rows, :])
            return fields[index][z, rows, :]

        for z in range(deep):
            slopes = []
            for index in range(2):
                field = fields[index]
                here = field[z, rows, :]
                dz = cells(index, z + 1) - cells(index, z - 1)
                if block == 0:
                    edge = jnp.where(at[2], field[z, 0:1, :], y_lo[index, z : z + 1, :])
                    up = jnp.concatenate([edge, field[z, 0:7, :]], axis=0)
                else:
                    up = field[z, top - 1 : top + 7, :]
                if top + 8 == tall:
                    edge = jnp.where(at[3], field[z, tall - 1 : tall, :], y_hi[index, z : z + 1, :])
                    down = jnp.concatenate([field[z, top + 1 : tall, :], edge], axis=0)
                else:
                    down = field[z, top + 1 : top + 9, :]
                dy = down - up
                right = jnp.where(not_last, pltpu.roll(here, wide - 1, 1), 0.0)
                left = jnp.where(not_first, pltpu.roll(here, 1, 1), 0.0)
                outer = x_step[z * tall + top : z * tall + top + 8, index * wide : (index + 1) * wide]
                dx = right - left + outer
                slopes.append((here, dz, dy, dx))
            t, tz, ty, tx = slopes[0]
            m, mz, my, mx = slopes[1]
            t_sq = tz * tz + ty * ty + tx * tx
            m_sq = mz * mz + my * my + mx * mx
            t_inverse = lax.rsqrt(t_sq * 0.25 + 1.0)
            m_inverse = lax.rsqrt(m_sq * 0.25 + 1.0)
            t_rest = t_inverse * t_inverse
            m_rest = m_inverse * m_inverse
            lit = (tx * sun[0] + ty * sun[1] + tz * sun[2]) * t_inverse
            both = t * m
            linear = [
                (base[r] + w[r][0] * t)
                + (w[r][1] * m + w[r][5] * both)
                + (w[r][4] * lit - (w[r][2] * t_rest + w[r][3] * m_rest))
                for r in range(4)
            ]
            soft = jnp.maximum(linear[3], 0.0) + jnp.log(1.0 + jnp.exp(-jnp.abs(linear[3])))
            kept = jnp.exp(soft * veil[rows, z * wide : (z + 1) * wide])
            weight = (1.0 - kept) * through
            through = through * kept
            for r in range(3):
                sums[r] = sums[r] + weight * jnp.tanh(linear[r])
            sums[3] = sums[3] + weight
        for r in range(3):
            sums[r] = 0.5 * (sums[r] + sums[3])
        for j in range(4):
            for r in range(4):
                image[order[4 * block + j], 2 * r : 2 * r + 2, :] = sums[r][2 * j : 2 * j + 2]


def over_kernel(order, parts, frame):
    wide = parts.shape[2]
    row = lax.broadcasted_iota(jnp.int32, (8, wide), 0)
    through = jnp.ones((8, wide), F32)
    total = jnp.zeros((8, wide), F32)
    for z in range(parts.shape[0]):
        part = parts[order[z]]
        veil = jnp.where(row >= 6, part, 0.0)
        veil = veil + pltpu.roll(veil, 4, 0)
        veil = veil + pltpu.roll(veil, 2, 0)
        total = total + through * part
        through = through * (1.0 - veil)
    for r in range(4):
        frame[r] = total[2 * r : 2 * r + 2]


def on_device(heat, blend, filled, weights, light):
    deep, tall, wide = heat.shape
    depth_count = lax.axis_size("gz")
    spacing = 2.0 / (deep * depth_count)
    own = faces(heat, blend)
    halos = []
    for axis, lo, hi in (("gx", own[0], own[1]), ("gy", own[2], own[3]), ("gz", own[4], own[5])):
        count = lax.axis_size(axis)
        halos.append(lax.ppermute(hi, axis, [(i, i + 1) for i in range(count - 1)]))
        halos.append(lax.ppermute(lo, axis, [(i + 1, i) for i in range(count - 1)]))
    first = depth_count * 5 // 8
    group = [(first + i) % depth_count for i in range(depth_count)]
    order = [group.index(z) for z in range(depth_count)]
    smem = pl.BlockSpec(memory_space=pltpu.SMEM)
    vmem = pl.BlockSpec(memory_space=pltpu.VMEM)

    def brick(*refs):
        brick_kernel(spacing, order, *refs)

    def over(*refs):
        over_kernel(order, *refs)

    image = pl.pallas_call(
        brick,
        out_shape=jax.ShapeDtypeStruct((depth_count, 8, wide), F32),
        in_specs=[smem] * 2 + [vmem] * 11,
        scratch_shapes=[
            pltpu.VMEM((deep * tall, 2 * wide), F32),
            pltpu.VMEM((tall, deep * wide), F32),
        ],
        compiler_params=SMALL,
        name="brick",
    )(weights, light, heat, blend, filled.reshape(deep, tall), *halos, own[0], own[1])
    parts = lax.all_to_all(image, "gz", 0, 0, tiled=True, axis_index_groups=[group])
    return pl.pallas_call(
        over,
        out_shape=jax.ShapeDtypeStruct((4, tall // depth_count, wide), F32),
        compiler_params=SMALL,
        name="over",
    )(parts)


def solution(mesh):
    placed = (P("gz", "gy", "gx"), P("gz", "gy", "gx"), P("gz", "gy", "gx"), P(), P())
    return jax.shard_map(
        on_device,
        mesh=mesh,
        in_specs=placed,
        out_specs=P(None, ("gy", "gz"), "gx"),
        check_vma=False,
    )
```

time: 76.4 us -> 71.6 us (0.937)
  the two profiles are of different devices: /device:TPU:1 before, /device:TPU:24 now
where the time goes in v2:
time: 71.6 us; the launch traced here: 70.5 us
  blocking collectives  46.1 us (64%)
  starting transfers between devices  15.4 us (22%)
  waiting for transfers between devices  4.21 us (6%)
  Pallas kernels  2.79 us (4%)
  local copies, waits for them, and re-layouts  1.92 us (3%)
    all_to_all x1, blocking collectives, on_device(): lax.all_to_all(image, 'gz', 0, 0, tiled=True, axis_index_groups=[group])  46.1 us
    ppermute x3, starting transfers between devices, on_device(): halos.append(lax.ppermute(hi, axis, [(i, i + 1) for i in range(count - 1)]))  9.13 us
    ppermute x3, starting transfers between devices, on_device(): halos.append(lax.ppermute(lo, axis, [(i + 1, i) for i in range(count - 1)]))  6.23 us
    ppermute x3, waiting for transfers between devices, on_device(): halos.append(lax.ppermute(lo, axis, [(i + 1, i) for i in range(count - 1)]))  4.21 us
    unnamed x10, local copies, waits for them, and re-layouts  1.92 us
    pallas_call x1, Pallas kernels, on_device(): pl.pallas_call(brick, out_shape=jax.ShapeDtypeStruct((depth_count, 8, wid...  1.75 us
  transfers between devices with their start and end apart: 6, of which 1 were waited for; matrix products, arithmetic and copies ran while one was open for 0% of the time, Pallas kernels for 0%

profile of v2, /device:TPU:24, one launch (start us, length us, event | category | flops | bytes accessed | tf_op | source)
XLA Modules:
  0.0 70.5 jit_solution(13701494334498612838)
XLA Ops:
  0.0 0.0 copy-start
  0.0 0.9 %copy-done = f32[8,64,128]{2,1,0:T(8,128)S(1)} copy-done((f32[8,64,128]{2,1,0:T(8,128)S(1)}, f32[8,64,128]{2,1,0:T(8,128)}, u32[]{:S(2)}) %copy-start) | copy-done | bytes 262168
  1.0 0.0 copy-start.1
  1.0 0.9 %copy-done.1 = f32[8,64,128]{2,1,0:T(8,128)S(1)} copy-done((f32[8,64,128]{2,1,0:T(8,128)S(1)}, f32[8,64,128]{2,1,0:T(8,128)}, u32[]{:S(2)}) %copy-start.1) | copy-done | bytes 262168
  1.9 0.4 faces.1
  2.3 3.8 %collective-permute-start.4 = (f32[2,64,128]{2,1,0:T(8,128)S(1)}, f32[2,64,128]{2,1,0:T(8,128)S(1)}, u32[]{:S(2)}, u32[]{:S(2)}) collective-permute-start(f32[2,64,128]{2,1,0:T(8,128)S(1)} %get-tuple-element.15), channel_id=1, source_target_pairs={{0,1},{1,2},{2,3},{3,4},{4,5},{5,6},{6,7},{7,8},{8,9},{9,10},{10,1... | collective-permute-start | bytes 196616 | tf_op jit(solution)/shard_map/ppermute | solution.py:176
  6.1 1.3 %collective-permute-start.5 = (f32[2,64,128]{2,1,0:T(8,128)S(1)}, f32[2,64,128]{2,1,0:T(8,128)S(1)}, u32[]{:S(2)}, u32[]{:S(2)}) collective-permute-start(f32[2,64,128]{2,1,0:T(8,128)S(1)} %get-tuple-element.16), channel_id=1, source_target_pairs={{1,0},{2,1},{3,2},{4,3},{5,4},{6,5},{7,6},{8,7},{9,8},{10,9},{11,1... | collective-permute-start | bytes 196616 | tf_op jit(solution)/shard_map/ppermute | solution.py:177
  7.4 0.0 copy-start.2
  7.4 3.4 %collective-permute-start = (f32[2,512]{1,0:T(2,128)S(1)}, f32[2,512]{1,0:T(2,128)S(1)}, u32[]{:S(2)}, u32[]{:S(2)}) collective-permute-start(f32[2,512]{1,0:T(2,128)S(1)} %get-tuple-element.11.refs_12_), channel_id=1, source_target_pairs={{0,256},{256,512},{512,768},{1,257},{257,513},{513,769},{2,258},{2... | collective-permute-start | bytes 12296 | tf_op jit(solution)/shard_map/ppermute | solution.py:176
  10.8 1.9 %collective-permute-start.2 = (f32[2,8,128]{2,1,0:T(8,128)S(1)}, f32[2,8,128]{2,1,0:T(8,128)S(1)}, u32[]{:S(2)}, u32[]{:S(2)}) collective-permute-start(f32[2,8,128]{2,1,0:T(8,128)S(1)} %get-tuple-element.13), channel_id=1, source_target_pairs={{0,32},{32,64},{64,96},{96,128},{128,160},{160,192},{192,224},{1,3... | collective-permute-start | bytes 24584 | tf_op jit(solution)/shard_map/ppermute | solution.py:176
  12.8 0.0 copy-start.3
  12.8 3.6 %collective-permute-start.3 = (f32[2,8,128]{2,1,0:T(8,128)S(1)}, f32[2,8,128]{2,1,0:T(8,128)S(1)}, u32[]{:S(2)}, u32[]{:S(2)}) collective-permute-start(f32[2,8,128]{2,1,0:T(8,128)S(1)} %get-tuple-element.14), channel_id=1, source_target_pairs={{32,0},{64,32},{96,64},{128,96},{160,128},{192,160},{224,192},{33,... | collective-permute-start | bytes 24584 | tf_op jit(solution)/shard_map/ppermute | solution.py:177
  16.4 0.0 collective-permute-done.refs_5_
  16.4 0.0 copy-start.4
  16.5 1.3 %collective-permute-start.1 = (f32[2,512]{1,0:T(2,128)S(1)}, f32[2,512]{1,0:T(2,128)S(1)}, u32[]{:S(2)}, u32[]{:S(2)}) collective-permute-start(f32[2,512]{1,0:T(2,128)S(1)} %get-tuple-element.12.refs_11_), channel_id=1, source_target_pairs={{256,0},{512,256},{768,512},{257,1},{513,257},{769,513},{258,2},{5... | collective-permute-start | bytes 12296 | tf_op jit(solution)/shard_map/ppermute | solution.py:177
  17.8 4.2 %collective-permute-done.1.refs_6_ = f32[2,512]{1,0:T(2,128)S(1)} collective-permute-done((f32[2,512]{1,0:T(2,128)S(1)}, f32[2,512]{1,0:T(2,128)S(1)}, u32[]{:S(2)}, u32[]{:S(2)}) %collective-permute-start.1) | collective-permute-done | bytes 4128 | tf_op jit(solution)/shard_map/ppermute | solution.py:177
  22.0 0.0 collective-permute-done.2.refs_7_
  22.0 0.0 collective-permute-done.3.refs_8_
  22.0 0.0 collective-permute-done.4.refs_9_
  22.0 0.0 collective-permute-done.5.refs_10_
  22.0 0.0 copy-done.2
  22.0 0.0 copy-done.3
  22.0 0.0 copy-done.4
  22.0 1.7 %brick.1 = f32[32,8,128]{2,1,0:T(8,128)S(1)} custom-call(f32[4,7]{1,0:T(4,128)S(1)} %copy-done.3, f32[3]{0:T(128)S(1)} %copy-done.4, f32[8,64,128]{2,1,0:T(8,128)S(1)} %copy-done, f32[8,64,128]{2,1,0:T(8,128)S(1)} %copy-done.1, s32[8,64]{1,0:T(8,128)S(1)} %bitcast.1, f32[2,512]{1,0:T(2,128)S(1)} %collective-permute-done.refs_5_, ...), custom_call_target="tpu_custom_call" | custom-call | tf_op jit(solution)/shard_map/brick/pallas_call | solution.py:190
  23.8 46.1 %all_to_all.5.refs_0_ = f32[32,8,128]{2,1,0:T(8,128)S(1)} all-to-all(f32[32,8,128]{2,1,0:T(8,128)S(1)} %brick.1), channel_id=1, replica_groups={{20,21,22,23,24,25,26,27,28,29,30,31,0,1,2,3,4,5,6,7,8,9,10,11,12,13,14..., dimensions={0} | all-to-all | bytes 262144 | tf_op jit(solution)/shard_map/all_to_all | solution.py:201
  69.9 0.6 over.1
Async XLA Ops:
  0.0 0.9 %copy-start = (f32[8,64,128]{2,1,0:T(8,128)S(1)}, f32[8,64,128]{2,1,0:T(8,128)}, u32[]{:S(2)}) copy-start(f32[8,64,128]{2,1,0:T(8,128)} %refs_2_.1) | copy-start | bytes 786436
  1.0 0.9 %copy-start.1 = (f32[8,64,128]{2,1,0:T(8,128)S(1)}, f32[8,64,128]{2,1,0:T(8,128)}, u32[]{:S(2)}) copy-start(f32[8,64,128]{2,1,0:T(8,128)} %refs_3_.1) | copy-start | bytes 786436
  2.3 19.7 %collective-permute-start.4 = (f32[2,64,128]{2,1,0:T(8,128)S(1)}, f32[2,64,128]{2,1,0:T(8,128)S(1)}, u32[]{:S(2)}, u32[]{:S(2)}) collective-permute-start(f32[2,64,128]{2,1,0:T(8,128)S(1)} %get-tuple-element.15), channel_id=1, source_target_pairs={{0,1},{1,2},{2,3},{3,4},{4,5},{5,6},{6,7},{7,8},{8,9},{9,10},{10,1... | collective-permute-start | bytes 196616 | tf_op jit(solution)/shard_map/ppermute | solution.py:176
  6.1 15.8 %collective-permute-start.5 = (f32[2,64,128]{2,1,0:T(8,128)S(1)}, f32[2,64,128]{2,1,0:T(8,128)S(1)}, u32[]{:S(2)}, u32[]{:S(2)}) collective-permute-start(f32[2,64,128]{2,1,0:T(8,128)S(1)} %get-tuple-element.16), channel_id=1, source_target_pairs={{1,0},{2,1},{3,2},{4,3},{5,4},{6,5},{7,6},{8,7},{9,8},{10,9},{11,1... | collective-permute-start | bytes 196616 | tf_op jit(solution)/shard_map/ppermute | solution.py:177
  7.4 14.6 %copy-start.2 = (s32[8,64,1]{1,2,0:T(1,128)S(1)}, s32[8,64,1]{1,2,0:T(1,128)}, u32[]{:S(2)}) copy-start(s32[8,64,1]{1,2,0:T(1,128)} %param.7) | copy-start | bytes 6148
  7.4 9.0 %collective-permute-start = (f32[2,512]{1,0:T(2,128)S(1)}, f32[2,512]{1,0:T(2,128)S(1)}, u32[]{:S(2)}, u32[]{:S(2)}) collective-permute-start(f32[2,512]{1,0:T(2,128)S(1)} %get-tuple-element.11.refs_12_), channel_id=1, source_target_pairs={{0,256},{256,512},{512,768},{1,257},{257,513},{513,769},{2,258},{2... | collective-permute-start | bytes 12296 | tf_op jit(solution)/shard_map/ppermute | solution.py:176
  10.8 11.1 %collective-permute-start.2 = (f32[2,8,128]{2,1,0:T(8,128)S(1)}, f32[2,8,128]{2,1,0:T(8,128)S(1)}, u32[]{:S(2)}, u32[]{:S(2)}) collective-permute-start(f32[2,8,128]{2,1,0:T(8,128)S(1)} %get-tuple-element.13), channel_id=1, source_target_pairs={{0,32},{32,64},{64,96},{96,128},{128,160},{160,192},{192,224},{1,3... | collective-permute-start | bytes 24584 | tf_op jit(solution)/shard_map/ppermute | solution.py:176
  12.8 9.2 %copy-start.3 = (f32[4,7]{1,0:T(4,128)S(1)}, f32[4,7]{1,0:T(4,128)}, u32[]{:S(2)}) copy-start(f32[4,7]{1,0:T(4,128)} %refs_0_.1) | copy-start | bytes 340
  12.8 9.2 %collective-permute-start.3 = (f32[2,8,128]{2,1,0:T(8,128)S(1)}, f32[2,8,128]{2,1,0:T(8,128)S(1)}, u32[]{:S(2)}, u32[]{:S(2)}) collective-permute-start(f32[2,8,128]{2,1,0:T(8,128)S(1)} %get-tuple-element.14), channel_id=1, source_target_pairs={{32,0},{64,32},{96,64},{128,96},{160,128},{192,160},{224,192},{33,... | collective-permute-start | bytes 24584 | tf_op jit(solution)/shard_map/ppermute | solution.py:177
  16.4 5.6 %copy-start.4 = (f32[3]{0:T(128)S(1)}, f32[3]{0:T(128)}, u32[]{:S(2)}) copy-start(f32[3]{0:T(128)} %refs_1_.1) | copy-start | bytes 40
  16.5 5.5 %collective-permute-start.1 = (f32[2,512]{1,0:T(2,128)S(1)}, f32[2,512]{1,0:T(2,128)S(1)}, u32[]{:S(2)}, u32[]{:S(2)}) collective-permute-start(f32[2,512]{1,0:T(2,128)S(1)} %get-tuple-element.12.refs_11_), channel_id=1, source_target_pairs={{256,0},{512,256},{768,512},{257,1},{513,257},{769,513},{258,2},{5... | collective-permute-start | bytes 12296 | tf_op jit(solution)/shard_map/ppermute | solution.py:177

commit v3 on v2

--- a/solution.py
+++ b/solution.py
@@ -9,37 +9,63 @@
 SMALL = pltpu.CompilerParams(vmem_limit_bytes=8 * 2**20)
 
 
-def face_kernel(heat, blend, x_lo, x_hi, y_lo, y_hi, z_lo, z_hi):
-    deep, tall, wide = heat.shape
-    for index, field in enumerate((heat, blend)):
-        z_lo[index] = field[0]
-        z_hi[index] = field[deep - 1]
-        y_lo[index] = jnp.concatenate([field[z, 0:1, :] for z in range(deep)], axis=0)
-        y_hi[index] = jnp.concatenate([field[z, tall - 1 : tall, :] for z in range(deep)], axis=0)
+def odd_place(axis):
+    return lax.axis_index(axis) % 2 == 1
+
+
+def face_kernel(far_heat, far_blend, heat, blend, x_a, x_b, y_a, y_b, z_a, z_b, arrived):
+    deep, tall, wide = heat.shape
+    halves = [slice(0, deep // 2), slice(deep // 2, deep)]
+    copies = [
+        [
+            pltpu.make_async_copy(far.at[half], near.at[half], arrived.at[2 * h + f])
+            for f, (far, near) in enumerate(((far_heat, heat), (far_blend, blend)))
+        ]
+        for h, half in enumerate(halves)
+    ]
+    for pair in copies:
+        for copy in pair:
+            copy.start()
+    odd_x, odd_y, odd_z = [odd_place(axis) for axis in ("gx", "gy", "gz")]
     lane = lax.broadcasted_iota(jnp.int32, (wide, wide), 1)
     slabs = wide // tall
-    for part in range(deep * tall // wide):
+    parts = deep * tall // wide
+    for part in range(parts):
+        if part % (parts // 2) == 0:
+            for copy in copies[part // (parts // 2)]:
+                copy.wait()
         t = heat[slabs * part : slabs * (part + 1)].reshape(wide, wide)
         m = blend[slabs * part : slabs * (part + 1)].reshape(wide, wide)
         ends = jnp.where(lane == 0, t, pltpu.roll(t, 2, 1))
         more = jnp.where(lane == 2, pltpu.roll(m, 2, 1), pltpu.roll(m, 4, 1))
         turned = jnp.where(lane < 2, ends, more).T
         here = slice(wide * part, wide * (part + 1))
-        x_lo[0:1, here] = turned[0:1]
-        x_hi[0:1, here] = turned[1:2]
-        x_lo[1:2, here] = turned[2:3]
-        x_hi[1:2, here] = turned[3:4]
+        for f in range(2):
+            low, high = turned[2 * f : 2 * f + 1], turned[2 * f + 1 : 2 * f + 2]
+            x_a[f : f + 1, here] = jnp.where(odd_x, low, high)
+            x_b[f : f + 1, here] = jnp.where(odd_x, high, low)
+    for f, field in enumerate((heat, blend)):
+        low, high = field[0], field[deep - 1]
+        z_a[f] = jnp.where(odd_z, low, high)
+        z_b[f] = jnp.where(odd_z, high, low)
+        low = jnp.concatenate([field[z, 0:1, :] for z in range(deep)], axis=0)
+        high = jnp.concatenate([field[z, tall - 1 : tall, :] for z in range(deep)], axis=0)
+        y_a[f] = jnp.where(odd_y, low, high)
+        y_b[f] = jnp.where(odd_y, high, low)
 
 
 def faces(heat, blend):
     deep, tall, wide = heat.shape
-    shapes = [(2, deep * tall)] * 2 + [(2, deep, wide)] * 2 + [(2, tall, wide)] * 2
+    shapes = [heat.shape] * 2
+    shapes += [(2, deep * tall)] * 2 + [(2, deep, wide)] * 2 + [(2, tall, wide)] * 2
     return pl.pallas_call(
         face_kernel,
         out_shape=[jax.ShapeDtypeStruct(s, F32) for s in shapes],
+        in_specs=[pl.BlockSpec(memory_space=pltpu.HBM)] * 2,
+        scratch_shapes=[pltpu.SemaphoreType.DMA((4,))],
         compiler_params=SMALL,
         name="faces",
-    )(heat, blend)
+    )(pltpu.with_memory_space_constraint(heat, pltpu.HBM), pltpu.with_memory_space_constraint(blend, pltpu.HBM))
 
 
 def split3(values):
@@ -50,16 +76,17 @@
 
 
 def brick_kernel(
-    spacing, order, weights, light, heat, blend, filled, x_lo, x_hi, y_lo, y_hi, z_lo, z_hi,
-    x_own_lo, x_own_hi, image, x_step, veil,
+    spacing, order, weights, light, heat, blend, filled, x_a, x_b, y_a, y_b, z_a, z_b,
+    x_own_b, image, x_step, veil,
 ):
     deep, tall, wide = heat.shape
     at = []
     for axis in ("gx", "gy", "gz"):
         at += [lax.axis_index(axis) == 0, lax.axis_index(axis) == lax.axis_size(axis) - 1]
-    below = jnp.where(at[0], x_own_lo[...], x_lo[...])
-    above = jnp.where(at[1], x_own_hi[...], x_hi[...])
-    sides = jnp.concatenate([below, above, jnp.zeros((4, deep * tall), F32)], axis=0)
+    odd_x, odd_y, odd_z = [odd_place(axis) for axis in ("gx", "gy", "gz")]
+    first = jnp.where(at[0], x_own_b[...], jnp.where(odd_x, x_a[...], x_b[...]))
+    last = jnp.where(at[1], x_own_b[...], jnp.where(odd_x, x_b[...], x_a[...]))
+    sides = jnp.concatenate([first, last, jnp.zeros((4, deep * tall), F32)], axis=0)
     sides = jnp.concatenate(split3(sides) + [jnp.zeros_like(sides)], axis=0).astype(jnp.bfloat16)
     row = lax.broadcasted_iota(jnp.int32, (32, 2 * wide), 0)
     side = row % 8
@@ -92,9 +119,11 @@
 
         def cells(index, z):
             if z < 0:
-                return jnp.where(at[4], fields[index][0, rows, :], z_lo[index, rows, :])
+                other = jnp.where(odd_z, z_a[index, rows, :], z_b[index, rows, :])
+                return jnp.where(at[4], fields[index][0, rows, :], other)
             if z == deep:
-                return jnp.where(at[5], fields[index][deep - 1, rows, :], z_hi[index, rows, :])
+                other = jnp.where(odd_z, z_b[index, rows, :], z_a[index, rows, :])
+                return jnp.where(at[5], fields[index][deep - 1, rows, :], other)
             return fields[index][z, rows, :]
 
         for z in range(deep):
@@ -104,12 +133,14 @@
                 here = field[z, rows, :]
                 dz = cells(index, z + 1) - cells(index, z - 1)
                 if block == 0:
-                    edge = jnp.where(at[2], field[z, 0:1, :], y_lo[index, z : z + 1, :])
+                    edge = jnp.where(odd_y, y_a[index, z : z + 1, :], y_b[index, z : z + 1, :])
+                    edge = jnp.where(at[2], field[z, 0:1, :], edge)
                     up = jnp.concatenate([edge, field[z, 0:7, :]], axis=0)
                 else:
                     up = field[z, top - 1 : top + 7, :]
                 if top + 8 == tall:
-                    edge = jnp.where(at[3], field[z, tall - 1 : tall, :], y_hi[index, z : z + 1, :])
+                    edge = jnp.where(odd_y, y_b[index, z : z + 1, :], y_a[index, z : z + 1, :])
+                    edge = jnp.where(at[3], field[z, tall - 1 : tall, :], edge)
                     down = jnp.concatenate([field[z, top + 1 : tall, :], edge], axis=0)
                 else:
                     down = field[z, top + 1 : top + 9, :]
@@ -169,12 +200,12 @@
     deep, tall, wide = heat.shape
     depth_count = lax.axis_size("gz")
     spacing = 2.0 / (deep * depth_count)
-    own = faces(heat, blend)
+    heat, blend, *own = faces(heat, blend)
     halos = []
-    for axis, lo, hi in (("gx", own[0], own[1]), ("gy", own[2], own[3]), ("gz", own[4], own[5])):
+    for axis, a, b in (("gx", own[0], own[1]), ("gy", own[2], own[3]), ("gz", own[4], own[5])):
         count = lax.axis_size(axis)
-        halos.append(lax.ppermute(hi, axis, [(i, i + 1) for i in range(count - 1)]))
-        halos.append(lax.ppermute(lo, axis, [(i + 1, i) for i in range(count - 1)]))
+        halos.append(lax.ppermute(a, axis, [(i, i ^ 1) for i in range(count)]))
+        halos.append(lax.ppermute(b, axis, [(i, ((i + 1) ^ 1) - 1) for i in range(1, count - 1)]))
     first = depth_count * 5 // 8
     group = [(first + i) % depth_count for i in range(depth_count)]
     order = [group.index(z) for z in range(depth_count)]
@@ -190,14 +221,14 @@
     image = pl.pallas_call(
         brick,
         out_shape=jax.ShapeDtypeStruct((depth_count, 8, wide), F32),
-        in_specs=[smem] * 2 + [vmem] * 11,
+        in_specs=[smem] * 2 + [vmem] * 10,
         scratch_shapes=[
             pltpu.VMEM((deep * tall, 2 * wide), F32),
             pltpu.VMEM((tall, deep * wide), F32),
         ],
         compiler_params=SMALL,
         name="brick",
-    )(weights, light, heat, blend, filled.reshape(deep, tall), *halos, own[0], own[1])
+    )(weights, light, heat, blend, filled.reshape(deep, tall), *halos, own[1])
     parts = lax.all_to_all(image, "gz", 0, 0, tiled=True, axis_index_groups=[group])
     return pl.pallas_call(
         over,

time: 71.6 us -> 71.2 us (level)
  the two profiles are of different devices: /device:TPU:24 before, /device:TPU:12 now
where the time goes in v3:
time: 71.2 us; the launch traced here: 70.8 us
  blocking collectives  40.1 us (56%)
  starting transfers between devices  24.5 us (34%)
  Pallas kernels  3.91 us (5%)
  waiting for transfers between devices  1.58 us (2%)
    all_to_all x1, blocking collectives, on_device(): lax.all_to_all(image, 'gz', 0, 0, tiled=True, axis_index_groups=[group])  40.1 us
    ppermute x3, starting transfers between devices, on_device(): lax.ppermute(b, axis, [(i, (i + 1 ^ 1) - 1) for i in range(1, count - 1)])  15.7 us
    ppermute x3, starting transfers between devices, on_device(): halos.append(lax.ppermute(a, axis, [(i, i ^ 1) for i in range(count)]))  8.85 us
    pallas_call x1, Pallas kernels, on_device(): pl.pallas_call(brick, out_shape=jax.ShapeDtypeStruct((depth_count, 8, wid...  1.77 us
    ppermute x3, waiting for transfers between devices, on_device(): lax.ppermute(b, axis, [(i, (i + 1 ^ 1) - 1) for i in range(1, count - 1)])  1.58 us
    pallas_call x1, Pallas kernels, faces(): pl.pallas_call(face_kernel, out_shape=[jax.ShapeDtypeStruct(s, F32) for s...  1.5 us
  transfers between devices with their start and end apart: 6, of which 1 were waited for; matrix products, arithmetic and copies ran while one was open for 0% of the time, Pallas kernels for 0%

profile of v3, /device:TPU:12, one launch (start us, length us, event | category | flops | bytes accessed | tf_op | source)
XLA Modules:
  0.0 70.8 jit_solution(12345576052751333808)
XLA Ops:
  0.0 1.5 %faces.1 = (f32[8,64,128]{2,1,0:T(8,128)S(1)}, f32[8,64,128]{2,1,0:T(8,128)S(1)}, f32[2,512]{1,0:T(2,128)S(1)}, f32[2,512]{1,0:T(2,128)S(1)}, f32[2,8,128]{2,1,0...) custom-call(f32[8,64,128]{2,1,0:T(8,128)} %far_heat.1, ...), custom_call_target="tpu_custom_call" | custom-call | tf_op jit(solution)/shard_map/faces/pallas_call | solution.py:61
  1.5 3.8 %collective-permute-start.4 = (f32[2,64,128]{2,1,0:T(8,128)S(1)}, f32[2,64,128]{2,1,0:T(8,128)S(1)}, u32[]{:S(2)}, u32[]{:S(2)}) collective-permute-start(f32[2,64,128]{2,1,0:T(8,128)S(1)} %get-tuple-element.19), channel_id=1, source_target_pairs={{0,1},{1,0},{2,3},{3,2},{4,5},{5,4},{6,7},{7,6},{8,9},{9,8},{10,11... | collective-permute-start | bytes 196616 | tf_op jit(solution)/shard_map/ppermute | solution.py:207
  5.3 0.7 collective-permute-start.5
  6.0 3.1 %collective-permute-start = (f32[2,512]{1,0:T(2,128)S(1)}, f32[2,512]{1,0:T(2,128)S(1)}, u32[]{:S(2)}, u32[]{:S(2)}) collective-permute-start(f32[2,512]{1,0:T(2,128)S(1)} %get-tuple-element.15), channel_id=1, source_target_pairs={{0,256},{256,0},{512,768},{768,512},{1,257},{257,1},{513,769},{769... | collective-permute-start | bytes 12296 | tf_op jit(solution)/shard_map/ppermute | solution.py:207
  9.1 1.9 %collective-permute-start.2 = (f32[2,8,128]{2,1,0:T(8,128)S(1)}, f32[2,8,128]{2,1,0:T(8,128)S(1)}, u32[]{:S(2)}, u32[]{:S(2)}) collective-permute-start(f32[2,8,128]{2,1,0:T(8,128)S(1)} %get-tuple-element.17), channel_id=1, source_target_pairs={{0,32},{32,0},{64,96},{96,64},{128,160},{160,128},{192,224},{224,1... | collective-permute-start | bytes 24584 | tf_op jit(solution)/shard_map/ppermute | solution.py:207
  11.1 0.0 copy-start
  11.1 2.5 %collective-permute-start.3 = (f32[2,8,128]{2,1,0:T(8,128)S(1)}, f32[2,8,128]{2,1,0:T(8,128)S(1)}, u32[]{:S(2)}, u32[]{:S(2)}) collective-permute-start(f32[2,8,128]{2,1,0:T(8,128)S(1)} %get-tuple-element.18), channel_id=1, source_target_pairs={{32,64},{64,32},{96,128},{128,96},{160,192},{192,160},{33,65},{65,... | collective-permute-start | bytes 24584 | tf_op jit(solution)/shard_map/ppermute | solution.py:208
  13.5 0.0 collective-permute-done.refs_5_
  13.6 12.5 %collective-permute-start.1 = (f32[2,512]{1,0:T(2,128)S(1)}, f32[2,512]{1,0:T(2,128)S(1)}, u32[]{:S(2)}, u32[]{:S(2)}) collective-permute-start(f32[2,512]{1,0:T(2,128)S(1)} %get-tuple-element.16.refs_11_), channel_id=1, source_target_pairs={{256,512},{512,256},{257,513},{513,257},{258,514},{514,258},{259,5... | collective-permute-start | bytes 12296 | tf_op jit(solution)/shard_map/ppermute | solution.py:208
  26.1 1.6 %collective-permute-done.1.refs_6_ = f32[2,512]{1,0:T(2,128)S(1)} collective-permute-done((f32[2,512]{1,0:T(2,128)S(1)}, f32[2,512]{1,0:T(2,128)S(1)}, u32[]{:S(2)}, u32[]{:S(2)}) %collective-permute-start.1) | collective-permute-done | bytes 4128 | tf_op jit(solution)/shard_map/ppermute | solution.py:208
  27.7 0.0 collective-permute-done.2.refs_7_
  27.7 0.0 collective-permute-done.3.refs_8_
  27.7 0.0 collective-permute-done.4.refs_9_
  27.7 0.0 collective-permute-done.5.refs_10_
  27.7 0.0 copy-start.1
  27.7 0.0 copy-start.2
  27.7 0.0 copy-done
  27.7 0.7 copy-done.1
  28.4 0.0 copy-done.2
  28.4 1.8 %brick.1 = f32[32,8,128]{2,1,0:T(8,128)S(1)} custom-call(f32[4,7]{1,0:T(4,128)S(1)} %copy-done.1, f32[3]{0:T(128)S(1)} %copy-done.2, f32[8,64,128]{2,1,0:T(8,128)S(1)} %get-tuple-element.13.refs_2_, f32[8,64,128]{2,1,0:T(8,128)S(1)} %get-tuple-element.14.refs_3_, s32[8,64]{1,0:T(8,128)S(1)} %bitcast.1, f32[2,512]{1,0:T(2,128)S(1)} %collective-permute-done.refs_5_, ...), custom_call_target="tpu_custom_call" | custom-call | tf_op jit(solution)/shard_map/brick/pallas_call | solution.py:221
  30.1 40.1 %all_to_all.5.refs_0_ = f32[32,8,128]{2,1,0:T(8,128)S(1)} all-to-all(f32[32,8,128]{2,1,0:T(8,128)S(1)} %brick.1), channel_id=1, replica_groups={{20,21,22,23,24,25,26,27,28,29,30,31,0,1,2,3,4,5,6,7,8,9,10,11,12,13,14..., dimensions={0} | all-to-all | bytes 262144 | tf_op jit(solution)/shard_map/all_to_all | solution.py:232
  70.2 0.6 over.1
Async XLA Ops:
  1.5 26.2 %collective-permute-start.4 = (f32[2,64,128]{2,1,0:T(8,128)S(1)}, f32[2,64,128]{2,1,0:T(8,128)S(1)}, u32[]{:S(2)}, u32[]{:S(2)}) collective-permute-start(f32[2,64,128]{2,1,0:T(8,128)S(1)} %get-tuple-element.19), channel_id=1, source_target_pairs={{0,1},{1,0},{2,3},{3,2},{4,5},{5,4},{6,7},{7,6},{8,9},{9,8},{10,11... | collective-permute-start | bytes 196616 | tf_op jit(solution)/shard_map/ppermute | solution.py:207
  5.3 22.3 %collective-permute-start.5 = (f32[2,64,128]{2,1,0:T(8,128)S(1)}, f32[2,64,128]{2,1,0:T(8,128)S(1)}, u32[]{:S(2)}, u32[]{:S(2)}) collective-permute-start(f32[2,64,128]{2,1,0:T(8,128)S(1)} %get-tuple-element.20), channel_id=1, source_target_pairs={{1,2},{2,1},{3,4},{4,3},{5,6},{6,5},{7,8},{8,7},{9,10},{10,9},{11,... | collective-permute-start | bytes 196616 | tf_op jit(solution)/shard_map/ppermute | solution.py:208
  6.0 7.5 %collective-permute-start = (f32[2,512]{1,0:T(2,128)S(1)}, f32[2,512]{1,0:T(2,128)S(1)}, u32[]{:S(2)}, u32[]{:S(2)}) collective-permute-start(f32[2,512]{1,0:T(2,128)S(1)} %get-tuple-element.15), channel_id=1, source_target_pairs={{0,256},{256,0},{512,768},{768,512},{1,257},{257,1},{513,769},{769... | collective-permute-start | bytes 12296 | tf_op jit(solution)/shard_map/ppermute | solution.py:207
  9.1 18.5 %collective-permute-start.2 = (f32[2,8,128]{2,1,0:T(8,128)S(1)}, f32[2,8,128]{2,1,0:T(8,128)S(1)}, u32[]{:S(2)}, u32[]{:S(2)}) collective-permute-start(f32[2,8,128]{2,1,0:T(8,128)S(1)} %get-tuple-element.17), channel_id=1, source_target_pairs={{0,32},{32,0},{64,96},{96,64},{128,160},{160,128},{192,224},{224,1... | collective-permute-start | bytes 24584 | tf_op jit(solution)/shard_map/ppermute | solution.py:207
  11.1 16.6 %copy-start = (s32[8,64,1]{1,2,0:T(1,128)S(1)}, s32[8,64,1]{1,2,0:T(1,128)}, u32[]{:S(2)}) copy-start(s32[8,64,1]{1,2,0:T(1,128)} %param.7) | copy-start | bytes 6148
  11.1 16.6 %collective-permute-start.3 = (f32[2,8,128]{2,1,0:T(8,128)S(1)}, f32[2,8,128]{2,1,0:T(8,128)S(1)}, u32[]{:S(2)}, u32[]{:S(2)}) collective-permute-start(f32[2,8,128]{2,1,0:T(8,128)S(1)} %get-tuple-element.18), channel_id=1, source_target_pairs={{32,64},{64,32},{96,128},{128,96},{160,192},{192,160},{33,65},{65,... | collective-permute-start | bytes 24584 | tf_op jit(solution)/shard_map/ppermute | solution.py:208
  13.6 14.1 %collective-permute-start.1 = (f32[2,512]{1,0:T(2,128)S(1)}, f32[2,512]{1,0:T(2,128)S(1)}, u32[]{:S(2)}, u32[]{:S(2)}) collective-permute-start(f32[2,512]{1,0:T(2,128)S(1)} %get-tuple-element.16.refs_11_), channel_id=1, source_target_pairs={{256,512},{512,256},{257,513},{513,257},{258,514},{514,258},{259,5... | collective-permute-start | bytes 12296 | tf_op jit(solution)/shard_map/ppermute | solution.py:208
  27.7 0.7 copy-start.1
  27.7 0.7 copy-start.2

commit v4 on v3

--- a/solution.py
+++ b/solution.py
@@ -9,11 +9,28 @@
 SMALL = pltpu.CompilerParams(vmem_limit_bytes=8 * 2**20)
 
 
+def in_hbm(array):
+    return pltpu.with_memory_space_constraint(array, pltpu.HBM)
+
+
 def odd_place(axis):
     return lax.axis_index(axis) % 2 == 1
 
 
-def face_kernel(far_heat, far_blend, heat, blend, x_a, x_b, y_a, y_b, z_a, z_b, arrived):
+def seat(column, core, columns):
+    return lax.rem(column + columns - 1, columns) * 2 + 1 - core
+
+
+def seats(columns, rows):
+    return [
+        [(i + 1) % columns * rows + 2 * chip + core for i in range(columns) for core in (1, 0)]
+        for chip in range(rows // 2)
+    ]
+
+
+def face_kernel(
+    far_heat, far_blend, heat, blend, flat, x_own, y_b, z_a, z_b, x_faces, arrived
+):
     deep, tall, wide = heat.shape
     halves = [slice(0, deep // 2), slice(deep // 2, deep)]
     copies = [
@@ -26,7 +43,8 @@
     for pair in copies:
         for copy in pair:
             copy.start()
-    odd_x, odd_y, odd_z = [odd_place(axis) for axis in ("gx", "gy", "gz")]
+    x_faces[...] = jnp.zeros_like(x_faces)
+    odd_y, odd_z = odd_place("gy"), odd_place("gz")
     lane = lax.broadcasted_iota(jnp.int32, (wide, wide), 1)
     slabs = wide // tall
     parts = deep * tall // wide
@@ -39,33 +57,42 @@
         ends = jnp.where(lane == 0, t, pltpu.roll(t, 2, 1))
         more = jnp.where(lane == 2, pltpu.roll(m, 2, 1), pltpu.roll(m, 4, 1))
         turned = jnp.where(lane < 2, ends, more).T
-        here = slice(wide * part, wide * (part + 1))
         for f in range(2):
-            low, high = turned[2 * f : 2 * f + 1], turned[2 * f + 1 : 2 * f + 2]
-            x_a[f : f + 1, here] = jnp.where(odd_x, low, high)
-            x_b[f : f + 1, here] = jnp.where(odd_x, high, low)
+            for side in range(2):
+                at = 2 * f + side
+                x_faces[side, f, part : part + 1, :] = turned[at : at + 1]
+    column, columns = lax.axis_index("gx"), lax.axis_size("gx")
+    core = lax.axis_index("gy") % 2
     for f, field in enumerate((heat, blend)):
         low, high = field[0], field[deep - 1]
         z_a[f] = jnp.where(odd_z, low, high)
         z_b[f] = jnp.where(odd_z, high, low)
         low = jnp.concatenate([field[z, 0:1, :] for z in range(deep)], axis=0)
         high = jnp.concatenate([field[z, tall - 1 : tall, :] for z in range(deep)], axis=0)
-        y_a[f] = jnp.where(odd_y, low, high)
         y_b[f] = jnp.where(odd_y, high, low)
+        beside = jnp.where(odd_y, low, high)
+        left, right = x_faces[0, f], x_faces[1, f]
+        x_own[f] = jnp.where(column == 0, left, right)
+        for i in range(columns):
+            other = (i + 1) % columns
+            along = jnp.where(column < other, right, left)
+            for place, its in ((2 * i, 1), (2 * i + 1, 0)):
+                flat[place, f] = jnp.where(core == its, along, beside)
 
 
 def faces(heat, blend):
     deep, tall, wide = heat.shape
-    shapes = [heat.shape] * 2
-    shapes += [(2, deep * tall)] * 2 + [(2, deep, wide)] * 2 + [(2, tall, wide)] * 2
+    members = 2 * lax.axis_size("gx")
+    shapes = [heat.shape] * 2 + [(members, 2, deep, wide)] + [(2, deep, wide)] * 2
+    shapes += [(2, tall, wide)] * 2
     return pl.pallas_call(
         face_kernel,
         out_shape=[jax.ShapeDtypeStruct(s, F32) for s in shapes],
         in_specs=[pl.BlockSpec(memory_space=pltpu.HBM)] * 2,
-        scratch_shapes=[pltpu.SemaphoreType.DMA((4,))],
+        scratch_shapes=[pltpu.VMEM((2, 2, deep, wide), F32), pltpu.SemaphoreType.DMA((4,))],
         compiler_params=SMALL,
         name="faces",
-    )(pltpu.with_memory_space_constraint(heat, pltpu.HBM), pltpu.with_memory_space_constraint(blend, pltpu.HBM))
+    )(in_hbm(heat), in_hbm(blend))
 
 
 def split3(values):
@@ -76,17 +103,32 @@
 
 
 def brick_kernel(
-    spacing, order, weights, light, heat, blend, filled, x_a, x_b, y_a, y_b, z_a, z_b,
-    x_own_b, image, x_step, veil,
+    spacing, order, far_weights, far_light, heat, blend, filled, flat, x_own, y_b, z_a, z_b,
+    image, x_step, veil, weights, light, arrived,
 ):
     deep, tall, wide = heat.shape
+    copies = [
+        pltpu.make_async_copy(far_weights, weights, arrived.at[0]),
+        pltpu.make_async_copy(far_light, light, arrived.at[1]),
+    ]
+    for copy in copies:
+        copy.start()
     at = []
     for axis in ("gx", "gy", "gz"):
         at += [lax.axis_index(axis) == 0, lax.axis_index(axis) == lax.axis_size(axis) - 1]
-    odd_x, odd_y, odd_z = [odd_place(axis) for axis in ("gx", "gy", "gz")]
-    first = jnp.where(at[0], x_own_b[...], jnp.where(odd_x, x_a[...], x_b[...]))
-    last = jnp.where(at[1], x_own_b[...], jnp.where(odd_x, x_b[...], x_a[...]))
-    sides = jnp.concatenate([first, last, jnp.zeros((4, deep * tall), F32)], axis=0)
+    odd_y, odd_z = odd_place("gy"), odd_place("gz")
+    column, columns = lax.axis_index("gx"), lax.axis_size("gx")
+    core = lax.axis_index("gy") % 2
+    left = seat(lax.rem(column + columns - 1, columns), core, columns)
+    right = seat(lax.rem(column + 1, columns), core, columns)
+    y_a = flat.at[seat(column, 1 - core, columns)]
+    parts = deep * tall // wide
+    sides = []
+    for edge, place in ((at[0], left), (at[1], right)):
+        for f in range(2):
+            face = jnp.where(edge, x_own[f], flat[place, f])
+            sides.append(jnp.concatenate([face[p : p + 1] for p in range(parts)], axis=1))
+    sides = jnp.concatenate(sides + [jnp.zeros((4, deep * tall), F32)], axis=0)
     sides = jnp.concatenate(split3(sides) + [jnp.zeros_like(sides)], axis=0).astype(jnp.bfloat16)
     row = lax.broadcasted_iota(jnp.int32, (32, 2 * wide), 0)
     side = row % 8
@@ -103,6 +145,8 @@
     veil[...] = lax.dot_general(
         filled[...].astype(F32), same, across, preferred_element_type=F32
     ) * (-spacing)
+    for copy in copies:
+        copy.wait()
     half = [0.5, 0.5, 0.5, 1.0]
     w = [[weights[r, k] * half[r] for k in range(7)] for r in range(4)]
     base = [w[r][6] + w[r][2] + w[r][3] for r in range(4)]
@@ -180,62 +224,84 @@
                 image[order[4 * block + j], 2 * r : 2 * r + 2, :] = sums[r][2 * j : 2 * j + 2]
 
 
-def over_kernel(order, parts, frame):
-    wide = parts.shape[2]
+def over_kernel(order, parts, out):
+    count, rows, wide = parts.shape
     row = lax.broadcasted_iota(jnp.int32, (8, wide), 0)
-    through = jnp.ones((8, wide), F32)
-    total = jnp.zeros((8, wide), F32)
-    for z in range(parts.shape[0]):
-        part = parts[order[z]]
-        veil = jnp.where(row >= 6, part, 0.0)
-        veil = veil + pltpu.roll(veil, 4, 0)
-        veil = veil + pltpu.roll(veil, 2, 0)
-        total = total + through * part
-        through = through * (1.0 - veil)
-    for r in range(4):
-        frame[r] = total[2 * r : 2 * r + 2]
+    for top in range(0, rows, 8):
+        through = jnp.ones((8, wide), F32)
+        total = jnp.zeros((8, wide), F32)
+        for i in range(count):
+            part = parts[order[i], top : top + 8, :]
+            veil = jnp.where(row >= 6, part, 0.0)
+            veil = veil + pltpu.roll(veil, 4, 0)
+            veil = veil + pltpu.roll(veil, 2, 0)
+            total = total + through * part
+            through = through * (1.0 - veil)
+        if out.shape[0] == 4:
+            for r in range(4):
+                out[r] = total[2 * r : 2 * r + 2]
+        else:
+            out[top : top + 8, :] = total
+
+
+def over(parts, order, shape):
+    def kernel(*refs):
+        over_kernel(order, *refs)
+
+    return pl.pallas_call(
+        kernel, out_shape=jax.ShapeDtypeStruct(shape, F32), compiler_params=SMALL, name="over"
+    )(parts)
 
 
 def on_device(heat, blend, filled, weights, light):
     deep, tall, wide = heat.shape
     depth_count = lax.axis_size("gz")
     spacing = 2.0 / (deep * depth_count)
-    heat, blend, *own = faces(heat, blend)
-    halos = []
-    for axis, a, b in (("gx", own[0], own[1]), ("gy", own[2], own[3]), ("gz", own[4], own[5])):
-        count = lax.axis_size(axis)
-        halos.append(lax.ppermute(a, axis, [(i, i ^ 1) for i in range(count)]))
-        halos.append(lax.ppermute(b, axis, [(i, ((i + 1) ^ 1) - 1) for i in range(1, count - 1)]))
-    first = depth_count * 5 // 8
-    group = [(first + i) % depth_count for i in range(depth_count)]
-    order = [group.index(z) for z in range(depth_count)]
-    smem = pl.BlockSpec(memory_space=pltpu.SMEM)
+    heat, blend, flat, x_own, y_b, z_a, z_b = faces(heat, blend)
+    flat = lax.all_to_all(
+        flat, ("gx", "gy"), 0, 0, tiled=True,
+        axis_index_groups=seats(lax.axis_size("gx"), lax.axis_size("gy")),
+    )
+    swap = {
+        axis: [(i, ((i + 1) ^ 1) - 1) for i in range(1, lax.axis_size(axis) - 1)]
+        for axis in ("gy", "gz")
+    }
+    y_b = lax.ppermute(y_b, "gy", swap["gy"])
+    z_a = lax.ppermute(z_a, "gz", [(i, i ^ 1) for i in range(depth_count)])
+    z_b = lax.ppermute(z_b, "gz", swap["gz"])
+    near = 4
+    far = depth_count // near
+    turn = [(far // 2 + i) % far for i in range(far)]
+    far_order = [turn.index(i) for i in range(far)]
+    near_groups = [[near * i + k for k in range(near)] for i in range(far)]
+    far_groups = [[near * i + k for i in turn] for k in range(near)]
+    order = [(z % near) * far + far_order[z // near] for z in range(depth_count)]
+    hbm = pl.BlockSpec(memory_space=pltpu.HBM)
     vmem = pl.BlockSpec(memory_space=pltpu.VMEM)
 
     def brick(*refs):
         brick_kernel(spacing, order, *refs)
-
-    def over(*refs):
-        over_kernel(order, *refs)
 
     image = pl.pallas_call(
         brick,
         out_shape=jax.ShapeDtypeStruct((depth_count, 8, wide), F32),
-        in_specs=[smem] * 2 + [vmem] * 10,
+        in_specs=[hbm] * 2 + [vmem] * 8,
         scratch_shapes=[
             pltpu.VMEM((deep * tall, 2 * wide), F32),
             pltpu.VMEM((tall, deep * wide), F32),
+            pltpu.SMEM(weights.shape, F32),
+            pltpu.SMEM(light.shape, F32),
+            pltpu.SemaphoreType.DMA((2,)),
         ],
         compiler_params=SMALL,
         name="brick",
-    )(weights, light, heat, blend, filled.reshape(deep, tall), *halos, own[1])
-    parts = lax.all_to_all(image, "gz", 0, 0, tiled=True, axis_index_groups=[group])
-    return pl.pallas_call(
-        over,
-        out_shape=jax.ShapeDtypeStruct((4, tall // depth_count, wide), F32),
-        compiler_params=SMALL,
-        name="over",
-    )(parts)
+    )(in_hbm(weights), in_hbm(light), heat, blend, filled.reshape(deep, tall), flat, x_own, y_b, z_a, z_b)
+    parts = lax.all_to_all(image, "gz", 0, 0, tiled=True, axis_index_groups=near_groups)
+    joined = over(parts.reshape(near, far * 8, wide), list(range(near)), (far * 8, wide))
+    parts = lax.all_to_all(
+        joined.reshape(far, 8, wide), "gz", 0, 0, tiled=True, axis_index_groups=far_groups
+    )
+    return over(parts, far_order, (4, tall // depth_count, wide))
 
 
 def solution(mesh):

time: 71.2 us -> 67.8 us (0.952)
  the two profiles are of different devices: /device:TPU:12 before, /device:TPU:24 now
where the time goes in v4:
time: 67.8 us; the launch traced here: 66.7 us
  blocking collectives  47.8 us (71%)
  starting transfers between devices  11.6 us (17%)
  Pallas kernels  4.53 us (7%)
  waiting for transfers between devices  2.63 us (4%)
    all_to_all x1, blocking collectives, on_device(): lax.all_to_all(joined.reshape(far, 8, wide), 'gz', 0, 0, tiled=True, axis...  31.8 us
    all_to_all x1, blocking collectives, on_device(): lax.all_to_all(image, 'gz', 0, 0, tiled=True, axis_index_groups=near_groups)  16 us
    all_to_all x1, starting transfers between devices, on_device(): lax.all_to_all(flat, ('gx', 'gy'), 0, 0, tiled=True, axis_index_groups=se...  4.66 us
    ppermute x1, starting transfers between devices, on_device(): z_a = lax.ppermute(z_a, 'gz', [(i, i ^ 1) for i in range(depth_count)])  3.83 us
    ppermute x1, waiting for transfers between devices, on_device(): y_b = lax.ppermute(y_b, 'gy', swap['gy'])  2.62 us
    ppermute x1, starting transfers between devices, on_device(): y_b = lax.ppermute(y_b, 'gy', swap['gy'])  2.46 us
    pallas_call x1, Pallas kernels, faces(): pl.pallas_call(face_kernel, out_shape=[jax.ShapeDtypeStruct(s, F32) for s...  2.13 us
    pallas_call x1, Pallas kernels, on_device(): pl.pallas_call(brick, out_shape=jax.ShapeDtypeStruct((depth_count, 8, wid...  1.76 us
  transfers between devices with their start and end apart: 4, of which 1 were waited for; matrix products, arithmetic and copies ran while one was open for 0% of the time, Pallas kernels for 0%

profile of v4, /device:TPU:24, one launch (start us, length us, event | category | flops | bytes accessed | tf_op | source)
XLA Modules:
  0.0 66.7 jit_solution(13440996965518127412)
XLA Ops:
  0.0 2.1 %faces.1 = (f32[8,64,128]{2,1,0:T(8,128)S(1)}, f32[8,64,128]{2,1,0:T(8,128)S(1)}, f32[8,2,8,128]{3,2,1,0:T(8,128)}, f32[2,8,128]{2,1,0:T(8,128)S(1)}, f32[2,8,12...) custom-call(f32[8,64,128]{2,1,0:T(8,128)} %far_heat.1, f32[8,64,128]{2,1,0:T(8,128)} %far_blend.1), custom_call_target="tpu_custom_call" | custom-call | tf_op jit(solution)/shard_map/faces/pallas_call | solution.py:88
  2.1 3.8 %collective-permute-start.1 = (f32[2,64,128]{2,1,0:T(8,128)S(1)}, f32[2,64,128]{2,1,0:T(8,128)S(1)}, u32[]{:S(2)}, u32[]{:S(2)}) collective-permute-start(f32[2,64,128]{2,1,0:T(8,128)S(1)} %get-tuple-element.17), channel_id=1, source_target_pairs={{0,1},{1,0},{2,3},{3,2},{4,5},{5,4},{6,7},{7,6},{8,9},{9,8},{10,11... | collective-permute-start | bytes 196616 | tf_op jit(solution)/shard_map/ppermute | solution.py:270
  6.0 0.7 collective-permute-start.2
  6.6 4.7 %all-to-all-start = ((f32[8,2,8,128]{3,2,1,0:T(8,128)}), f32[8,2,8,128]{3,2,1,0:T(8,128)S(1)}, u32[]{:S(2)}, u32[]{:S(2)}) async-start(f32[8,2,8,128]{3,2,1,0:T(8,128)} %get-tuple-element.14), calls=%async_computation | async-start | bytes 131072 | tf_op jit(solution)/shard_map/all_to_all | solution.py:261
  11.3 0.0 copy-start
  11.3 2.5 %collective-permute-start = (f32[2,8,128]{2,1,0:T(8,128)S(1)}, f32[2,8,128]{2,1,0:T(8,128)S(1)}, u32[]{:S(2)}, u32[]{:S(2)}) collective-permute-start(f32[2,8,128]{2,1,0:T(8,128)S(1)} %get-tuple-element.16), channel_id=1, source_target_pairs={{32,64},{64,32},{96,128},{128,96},{160,192},{192,160},{33,65},{65,... | collective-permute-start | bytes 24584 | tf_op jit(solution)/shard_map/ppermute | solution.py:269
  13.8 2.6 %collective-permute-done.refs_7_ = f32[2,8,128]{2,1,0:T(8,128)S(1)} collective-permute-done((f32[2,8,128]{2,1,0:T(8,128)S(1)}, f32[2,8,128]{2,1,0:T(8,128)S(1)}, u32[]{:S(2)}, u32[]{:S(2)}) %collective-permute-start) | collective-permute-done | bytes 8224 | tf_op jit(solution)/shard_map/ppermute | solution.py:269
  16.4 0.0 all-to-all-done.refs_5_
  16.4 0.0 collective-permute-done.1.refs_8_
  16.4 0.0 collective-permute-done.2.refs_9_
  16.4 0.0 copy-done
  16.4 1.8 %brick.1 = f32[32,8,128]{2,1,0:T(8,128)S(1)} custom-call(f32[4,7]{1,0:T(4,128)} %refs_0_.1, f32[3]{0:T(128)} %refs_1_.1, f32[8,64,128]{2,1,0:T(8,128)S(1)} %get-tuple-element.12.refs_2_, f32[8,64,128]{2,1,0:T(8,128)S(1)} %get-tuple-element.13.refs_3_, s32[8,64]{1,0:T(8,128)S(1)} %bitcast.5, f32[8,2,8,128]{3,2,1,0:T(8,128)S(1)} %all-to-all-done.refs_5_, ...), custom_call_target="tpu_custom_call" | custom-call | tf_op jit(solution)/shard_map/brick/pallas_call | solution.py:285
  18.2 16.0 %all_to_all.15 = f32[32,8,128]{2,1,0:T(8,128)S(1)} all-to-all(f32[32,8,128]{2,1,0:T(8,128)S(1)} %brick.1), channel_id=1, replica_groups={{0,1,2,3},{4,5,6,7},{8,9,10,11},{12,13,14,15},{16,17,18,19},{20,21,22,2..., dimensions={0} | all-to-all | bytes 262144 | tf_op jit(solution)/shard_map/all_to_all | solution.py:299
  34.2 31.8 %all_to_all.16.refs_0_ = f32[8,8,128]{2,1,0:T(8,128)S(1)} all-to-all(f32[8,8,128]{2,1,0:T(8,128)S(1)} %bitcast.4), channel_id=1, replica_groups={{16,20,24,28,0,4,8,12},{17,21,25,29,1,5,9,13},{18,22,26,30,2,6,10,14},{..., dimensions={0} | all-to-all | bytes 65536 | tf_op jit(solution)/shard_map/all_to_all | solution.py:301
  66.0 0.6 over.3
  (1 shorter events, 0.0 us)
Async XLA Ops:
  2.1 14.3 %collective-permute-start.1 = (f32[2,64,128]{2,1,0:T(8,128)S(1)}, f32[2,64,128]{2,1,0:T(8,128)S(1)}, u32[]{:S(2)}, u32[]{:S(2)}) collective-permute-start(f32[2,64,128]{2,1,0:T(8,128)S(1)} %get-tuple-element.17), channel_id=1, source_target_pairs={{0,1},{1,0},{2,3},{3,2},{4,5},{5,4},{6,7},{7,6},{8,9},{9,8},{10,11... | collective-permute-start | bytes 196616 | tf_op jit(solution)/shard_map/ppermute | solution.py:270
  6.0 10.4 %collective-permute-start.2 = (f32[2,64,128]{2,1,0:T(8,128)S(1)}, f32[2,64,128]{2,1,0:T(8,128)S(1)}, u32[]{:S(2)}, u32[]{:S(2)}) collective-permute-start(f32[2,64,128]{2,1,0:T(8,128)S(1)} %get-tuple-element.18), channel_id=1, source_target_pairs={{1,2},{2,1},{3,4},{4,3},{5,6},{6,5},{7,8},{8,7},{9,10},{10,9},{11,... | collective-permute-start | bytes 196616 | tf_op jit(solution)/shard_map/ppermute | solution.py:271
  6.6 9.8 %all-to-all-start = ((f32[8,2,8,128]{3,2,1,0:T(8,128)}), f32[8,2,8,128]{3,2,1,0:T(8,128)S(1)}, u32[]{:S(2)}, u32[]{:S(2)}) async-start(f32[8,2,8,128]{3,2,1,0:T(8,128)} %get-tuple-element.14), calls=%async_computation | async-start | bytes 131072 | tf_op jit(solution)/shard_map/all_to_all | solution.py:261
  11.3 5.1 %copy-start = (s32[8,64,1]{1,2,0:T(1,128)S(1)}, s32[8,64,1]{1,2,0:T(1,128)}, u32[]{:S(2)}) copy-start(s32[8,64,1]{1,2,0:T(1,128)} %param.7) | copy-start | bytes 6148
  11.3 5.1 %collective-permute-start = (f32[2,8,128]{2,1,0:T(8,128)S(1)}, f32[2,8,128]{2,1,0:T(8,128)S(1)}, u32[]{:S(2)}, u32[]{:S(2)}) collective-permute-start(f32[2,8,128]{2,1,0:T(8,128)S(1)} %get-tuple-element.16), channel_id=1, source_target_pairs={{32,64},{64,32},{96,128},{128,96},{160,192},{192,160},{33,65},{65,... | collective-permute-start | bytes 24584 | tf_op jit(solution)/shard_map/ppermute | solution.py:269

commit v5 on v4

--- a/solution.py
+++ b/solution.py
@@ -77,13 +77,14 @@
             other = (i + 1) % columns
             along = jnp.where(column < other, right, left)
             for place, its in ((2 * i, 1), (2 * i + 1, 0)):
-                flat[place, f] = jnp.where(core == its, along, beside)
+                flat[place, f, 0:deep, :] = jnp.where(core == its, along, beside)
+                flat[place, f, deep:, :] = jnp.zeros((deep, wide), F32)
 
 
 def faces(heat, blend):
     deep, tall, wide = heat.shape
     members = 2 * lax.axis_size("gx")
-    shapes = [heat.shape] * 2 + [(members, 2, deep, wide)] + [(2, deep, wide)] * 2
+    shapes = [heat.shape] * 2 + [(members, 2, 2 * deep, wide)] + [(2, deep, wide)] * 2
     shapes += [(2, tall, wide)] * 2
     return pl.pallas_call(
         face_kernel,
@@ -103,7 +104,7 @@
 
 
 def brick_kernel(
-    spacing, order, far_weights, far_light, heat, blend, filled, flat, x_own, y_b, z_a, z_b,
+    spacing, order, far_weights, far_light, heat, blend, filled, flat, x_own, y_b, z_b, z_a,
     image, x_step, veil, weights, light, arrived,
 ):
     deep, tall, wide = heat.shape
@@ -126,7 +127,7 @@
     sides = []
     for edge, place in ((at[0], left), (at[1], right)):
         for f in range(2):
-            face = jnp.where(edge, x_own[f], flat[place, f])
+            face = jnp.where(edge, x_own[f], flat[place, f, 0:deep, :])
             sides.append(jnp.concatenate([face[p : p + 1] for p in range(parts)], axis=1))
     sides = jnp.concatenate(sides + [jnp.zeros((4, deep * tall), F32)], axis=0)
     sides = jnp.concatenate(split3(sides) + [jnp.zeros_like(sides)], axis=0).astype(jnp.bfloat16)
@@ -270,12 +271,14 @@
     z_a = lax.ppermute(z_a, "gz", [(i, i ^ 1) for i in range(depth_count)])
     z_b = lax.ppermute(z_b, "gz", swap["gz"])
     near = 4
+    near_turn = [2, 1, 0, 3]
     far = depth_count // near
     turn = [(far // 2 + i) % far for i in range(far)]
     far_order = [turn.index(i) for i in range(far)]
-    near_groups = [[near * i + k for k in range(near)] for i in range(far)]
+    near_order = [near_turn.index(k) for k in range(near)]
+    near_groups = [[near * i + k for k in near_turn] for i in range(far)]
     far_groups = [[near * i + k for i in turn] for k in range(near)]
-    order = [(z % near) * far + far_order[z // near] for z in range(depth_count)]
+    order = [near_order[z % near] * far + far_order[z // near] for z in range(depth_count)]
     hbm = pl.BlockSpec(memory_space=pltpu.HBM)
     vmem = pl.BlockSpec(memory_space=pltpu.VMEM)
 
@@ -295,9 +298,9 @@
         ],
         compiler_params=SMALL,
         name="brick",
-    )(in_hbm(weights), in_hbm(light), heat, blend, filled.reshape(deep, tall), flat, x_own, y_b, z_a, z_b)
+    )(in_hbm(weights), in_hbm(light), heat, blend, filled.reshape(deep, tall), flat, x_own, y_b, z_b, z_a)
     parts = lax.all_to_all(image, "gz", 0, 0, tiled=True, axis_index_groups=near_groups)
-    joined = over(parts.reshape(near, far * 8, wide), list(range(near)), (far * 8, wide))
+    joined = over(parts.reshape(near, far * 8, wide), near_order, (far * 8, wide))
     parts = lax.all_to_all(
         joined.reshape(far, 8, wide), "gz", 0, 0, tiled=True, axis_index_groups=far_groups
     )

time: 67.8 us -> 66 us (0.973); the launches traced: 66.7 us -> 65.7 us
  blocking collectives: 47.8 us -> 43.8 us
  starting transfers between devices: 11.6 us -> 14.2 us
    all_to_all x1, blocking collectives: 16 us -> 10.8 us  [on_device(): lax.all_to_all(image, 'gz', 0, 0, tiled=True, axis_index_groups=near_groups)]
    ppermute x1, starting transfers between devices: 3.83 us -> 6.99 us  [on_device(): z_a = lax.ppermute(z_a, 'gz', [(i, i ^ 1) for i in range(depth_count)])]
    all_to_all x1, blocking collectives: 31.8 us -> 33 us  [on_device(): lax.all_to_all(joined.reshape(far, 8, wide), 'gz', 0, 0, tiled=True, axis...]
where the time goes in v5:
time: 66 us; the launch traced here: 65.7 us
  blocking collectives  43.8 us (66%)
  starting transfers between devices  14.2 us (22%)
  Pallas kernels  4.55 us (7%)
  waiting for transfers between devices  3.05 us (5%)
    all_to_all x1, blocking collectives, on_device(): lax.all_to_all(joined.reshape(far, 8, wide), 'gz', 0, 0, tiled=True, axis...  33 us
    all_to_all x1, blocking collectives, on_device(): lax.all_to_all(image, 'gz', 0, 0, tiled=True, axis_index_groups=near_groups)  10.8 us
    ppermute x1, starting transfers between devices, on_device(): z_a = lax.ppermute(z_a, 'gz', [(i, i ^ 1) for i in range(depth_count)])  6.99 us
    all_to_all x1, starting transfers between devices, on_device(): lax.all_to_all(flat, ('gx', 'gy'), 0, 0, tiled=True, axis_index_groups=se...  4.66 us
    ppermute x1, waiting for transfers between devices, on_device(): y_b = lax.ppermute(y_b, 'gy', swap['gy'])  3.04 us
    pallas_call x1, Pallas kernels, faces(): pl.pallas_call(face_kernel, out_shape=[jax.ShapeDtypeStruct(s, F32) for s...  2.15 us
    ppermute x1, starting transfers between devices, on_device(): y_b = lax.ppermute(y_b, 'gy', swap['gy'])  1.92 us
    pallas_call x1, Pallas kernels, on_device(): pl.pallas_call(brick, out_shape=jax.ShapeDtypeStruct((depth_count, 8, wid...  1.76 us
  transfers between devices with their start and end apart: 4, of which 1 were waited for; matrix products, arithmetic and copies ran while one was open for 0% of the time, Pallas kernels for 0%

profile of v5, /device:TPU:24, one launch (start us, length us, event | category | flops | bytes accessed | tf_op | source)
XLA Modules:
  0.0 65.7 jit_solution(12360644836452578321)
XLA Ops:
  0.0 2.1 %faces.1 = (f32[8,64,128]{2,1,0:T(8,128)S(1)}, f32[8,64,128]{2,1,0:T(8,128)S(1)}, f32[8,2,16,128]{3,2,1,0:T(8,128)}, f32[2,8,128]{2,1,0:T(8,128)S(1)}, f32[2,8,1...) custom-call(f32[8,64,128]{2,1,0:T(8,128)} %far_heat.1, f32[8,64,128]{2,1,0:T(8,128)} %far_blend.1), custom_call_target="tpu_custom_call" | custom-call | tf_op jit(solution)/shard_map/faces/pallas_call | solution.py:89
  2.2 4.7 %all-to-all-start = ((f32[8,2,16,128]{3,2,1,0:T(8,128)}), f32[8,2,16,128]{3,2,1,0:T(8,128)S(1)}, u32[]{:S(2)}, u32[]{:S(2)}) async-start(f32[8,2,16,128]{3,2,1,0:T(8,128)} %get-tuple-element.14), calls=%async_computation | async-start | bytes 262144 | tf_op jit(solution)/shard_map/all_to_all | solution.py:262
  6.8 0.7 collective-permute-start.1
  7.5 7.0 %collective-permute-start.2 = (f32[2,64,128]{2,1,0:T(8,128)S(1)}, f32[2,64,128]{2,1,0:T(8,128)S(1)}, u32[]{:S(2)}, u32[]{:S(2)}) collective-permute-start(f32[2,64,128]{2,1,0:T(8,128)S(1)} %get-tuple-element.18), channel_id=1, source_target_pairs={{0,1},{1,0},{2,3},{3,2},{4,5},{5,4},{6,7},{7,6},{8,9},{9,8},{10,11... | collective-permute-start | bytes 196616 | tf_op jit(solution)/shard_map/ppermute | solution.py:271
  14.5 0.0 copy-start
  14.5 1.9 %collective-permute-start = (f32[2,8,128]{2,1,0:T(8,128)S(1)}, f32[2,8,128]{2,1,0:T(8,128)S(1)}, u32[]{:S(2)}, u32[]{:S(2)}) collective-permute-start(f32[2,8,128]{2,1,0:T(8,128)S(1)} %get-tuple-element.16), channel_id=1, source_target_pairs={{32,64},{64,32},{96,128},{128,96},{160,192},{192,160},{33,65},{65,... | collective-permute-start | bytes 24584 | tf_op jit(solution)/shard_map/ppermute | solution.py:270
  16.4 3.0 %collective-permute-done.refs_7_ = f32[2,8,128]{2,1,0:T(8,128)S(1)} collective-permute-done((f32[2,8,128]{2,1,0:T(8,128)S(1)}, f32[2,8,128]{2,1,0:T(8,128)S(1)}, u32[]{:S(2)}, u32[]{:S(2)}) %collective-permute-start) | collective-permute-done | bytes 8224 | tf_op jit(solution)/shard_map/ppermute | solution.py:270
  19.4 0.0 collective-permute-done.1.refs_8_
  19.5 0.0 collective-permute-done.2.refs_9_
  19.5 0.0 all-to-all-done.refs_5_
  19.5 0.0 copy-done
  19.5 1.8 %brick.1 = f32[32,8,128]{2,1,0:T(8,128)S(1)} custom-call(f32[4,7]{1,0:T(4,128)} %refs_0_.1, f32[3]{0:T(128)} %refs_1_.1, f32[8,64,128]{2,1,0:T(8,128)S(1)} %get-tuple-element.12.refs_2_, f32[8,64,128]{2,1,0:T(8,128)S(1)} %get-tuple-element.13.refs_3_, s32[8,64]{1,0:T(8,128)S(1)} %bitcast.5, f32[8,2,16,128]{3,2,1,0:T(8,128)S(1)} %all-to-all-done.refs_5_, ...), custom_call_target="tpu_custom_call" | custom-call | tf_op jit(solution)/shard_map/brick/pallas_call | solution.py:288
  21.2 10.8 %all_to_all.15 = f32[32,8,128]{2,1,0:T(8,128)S(1)} all-to-all(f32[32,8,128]{2,1,0:T(8,128)S(1)} %brick.1), channel_id=1, replica_groups={{2,1,0,3},{6,5,4,7},{10,9,8,11},{14,13,12,15},{18,17,16,19},{22,21,20,2..., dimensions={0} | all-to-all | bytes 262144 | tf_op jit(solution)/shard_map/all_to_all | solution.py:302
  32.1 33.0 %all_to_all.16.refs_0_ = f32[8,8,128]{2,1,0:T(8,128)S(1)} all-to-all(f32[8,8,128]{2,1,0:T(8,128)S(1)} %bitcast.4), channel_id=1, replica_groups={{16,20,24,28,0,4,8,12},{17,21,25,29,1,5,9,13},{18,22,26,30,2,6,10,14},{..., dimensions={0} | all-to-all | bytes 65536 | tf_op jit(solution)/shard_map/all_to_all | solution.py:304
  65.0 0.6 over.3
  (1 shorter events, 0.0 us)
Async XLA Ops:
  2.2 17.3 %all-to-all-start = ((f32[8,2,16,128]{3,2,1,0:T(8,128)}), f32[8,2,16,128]{3,2,1,0:T(8,128)S(1)}, u32[]{:S(2)}, u32[]{:S(2)}) async-start(f32[8,2,16,128]{3,2,1,0:T(8,128)} %get-tuple-element.14), calls=%async_computation | async-start | bytes 262144 | tf_op jit(solution)/shard_map/all_to_all | solution.py:262
  6.8 12.6 %collective-permute-start.1 = (f32[2,64,128]{2,1,0:T(8,128)S(1)}, f32[2,64,128]{2,1,0:T(8,128)S(1)}, u32[]{:S(2)}, u32[]{:S(2)}) collective-permute-start(f32[2,64,128]{2,1,0:T(8,128)S(1)} %get-tuple-element.17), channel_id=1, source_target_pairs={{1,2},{2,1},{3,4},{4,3},{5,6},{6,5},{7,8},{8,7},{9,10},{10,9},{11,... | collective-permute-start | bytes 196616 | tf_op jit(solution)/shard_map/ppermute | solution.py:272
  7.5 12.0 %collective-permute-start.2 = (f32[2,64,128]{2,1,0:T(8,128)S(1)}, f32[2,64,128]{2,1,0:T(8,128)S(1)}, u32[]{:S(2)}, u32[]{:S(2)}) collective-permute-start(f32[2,64,128]{2,1,0:T(8,128)S(1)} %get-tuple-element.18), channel_id=1, source_target_pairs={{0,1},{1,0},{2,3},{3,2},{4,5},{5,4},{6,7},{7,6},{8,9},{9,8},{10,11... | collective-permute-start | bytes 196616 | tf_op jit(solution)/shard_map/ppermute | solution.py:271
  14.5 5.0 %copy-start = (s32[8,64,1]{1,2,0:T(1,128)S(1)}, s32[8,64,1]{1,2,0:T(1,128)}, u32[]{:S(2)}) copy-start(s32[8,64,1]{1,2,0:T(1,128)} %param.7) | copy-start | bytes 6148
  14.5 5.0 %collective-permute-start = (f32[2,8,128]{2,1,0:T(8,128)S(1)}, f32[2,8,128]{2,1,0:T(8,128)S(1)}, u32[]{:S(2)}, u32[]{:S(2)}) collective-permute-start(f32[2,8,128]{2,1,0:T(8,128)S(1)} %get-tuple-element.16), channel_id=1, source_target_pairs={{32,64},{64,32},{96,128},{128,96},{160,192},{192,160},{33,65},{65,... | collective-permute-start | bytes 24584 | tf_op jit(solution)/shard_map/ppermute | solution.py:270

commit v6 on v5

--- a/solution.py
+++ b/solution.py
@@ -103,29 +103,44 @@
     return [high, middle, rest - middle]
 
 
-def brick_kernel(
-    spacing, order, far_weights, far_light, heat, blend, filled, flat, x_own, y_b, z_b, z_a,
-    image, x_step, veil, weights, light, arrived,
-):
-    deep, tall, wide = heat.shape
+def table(weights, light):
+    return [
+        pltpu.SMEM(weights.shape, F32),
+        pltpu.SMEM(light.shape, F32),
+        pltpu.SemaphoreType.DMA((4,)),
+    ]
+
+
+def fetch(far_weights, far_light, weights, light, arrived):
     copies = [
         pltpu.make_async_copy(far_weights, weights, arrived.at[0]),
         pltpu.make_async_copy(far_light, light, arrived.at[1]),
     ]
     for copy in copies:
         copy.start()
-    at = []
-    for axis in ("gx", "gy", "gz"):
-        at += [lax.axis_index(axis) == 0, lax.axis_index(axis) == lax.axis_size(axis) - 1]
-    odd_y, odd_z = odd_place("gy"), odd_place("gz")
+    return copies
+
+
+def edges(axis):
+    place = lax.axis_index(axis)
+    return [place == 0, place == lax.axis_size(axis) - 1]
+
+
+def inner_kernel(
+    spacing, order, far_weights, far_light, heat, blend, filled, flat, x_own, z_b, z_a,
+    image, x_step, veil, near_weights, near_light, weights, light, arrived,
+):
+    deep, tall, wide = heat.shape
+    copies = fetch(far_weights, far_light, weights, light, arrived)
+    copies += fetch(far_weights, far_light, near_weights, near_light, arrived.at[2:])
+    first, last = edges("gx")
     column, columns = lax.axis_index("gx"), lax.axis_size("gx")
     core = lax.axis_index("gy") % 2
     left = seat(lax.rem(column + columns - 1, columns), core, columns)
     right = seat(lax.rem(column + 1, columns), core, columns)
-    y_a = flat.at[seat(column, 1 - core, columns)]
     parts = deep * tall // wide
     sides = []
-    for edge, place in ((at[0], left), (at[1], right)):
+    for edge, place in ((first, left), (last, right)):
         for f in range(2):
             face = jnp.where(edge, x_own[f], flat[place, f, 0:deep, :])
             sides.append(jnp.concatenate([face[p : p + 1] for p in range(parts)], axis=1))
@@ -148,6 +163,31 @@
     ) * (-spacing)
     for copy in copies:
         copy.wait()
+    blocks = range(1, tall // 8 - 1)
+    rays(order, blocks, weights, light, heat, blend, None, None, z_a, z_b, x_step, veil, image)
+
+
+def outer_kernel(
+    order, far_weights, far_light, heat, blend, flat, y_b, z_b, z_a, part, x_step, veil,
+    image, weights, light, arrived,
+):
+    deep, tall, wide = heat.shape
+    copies = fetch(far_weights, far_light, weights, light, arrived)
+    last = tall // 8 - 1
+    for chunk in range(4, 4 * last):
+        image[order[chunk]] = part[order[chunk]]
+    core = lax.axis_index("gy") % 2
+    y_a = flat.at[seat(lax.axis_index("gx"), 1 - core, lax.axis_size("gx"))]
+    for copy in copies:
+        copy.wait()
+    blocks = (0, last)
+    rays(order, blocks, weights, light, heat, blend, y_a, y_b, z_a, z_b, x_step, veil, image)
+
+
+def rays(order, blocks, weights, light, heat, blend, y_a, y_b, z_a, z_b, x_step, veil, image):
+    deep, tall, wide = heat.shape
+    odd_y, odd_z = odd_place("gy"), odd_place("gz")
+    at = edges("gx") + edges("gy") + edges("gz")
     half = [0.5, 0.5, 0.5, 1.0]
     w = [[weights[r, k] * half[r] for k in range(7)] for r in range(4)]
     base = [w[r][6] + w[r][2] + w[r][3] for r in range(4)]
@@ -156,7 +196,7 @@
     lane8 = lax.broadcasted_iota(jnp.int32, (8, wide), 1)
     not_first = lane8 > 0
     not_last = lane8 < wide - 1
-    for block in range(tall // 8):
+    for block in blocks:
         top = 8 * block
         rows = slice(top, top + 8)
         through = jnp.ones((8, wide), F32)
@@ -282,23 +322,40 @@
     hbm = pl.BlockSpec(memory_space=pltpu.HBM)
     vmem = pl.BlockSpec(memory_space=pltpu.VMEM)
 
-    def brick(*refs):
-        brick_kernel(spacing, order, *refs)
-
+    def inner(*refs):
+        inner_kernel(spacing, order, *refs)
+
+    def outer(*refs):
+        outer_kernel(order, *refs)
+
+    weights, light = in_hbm(weights), in_hbm(light)
+    shape = jax.ShapeDtypeStruct((depth_count, 8, wide), F32)
+    cells = deep * tall * wide
+    part, x_step, veil, near_weights, near_light = pl.pallas_call(
+        inner,
+        out_shape=[
+            shape,
+            jax.ShapeDtypeStruct((deep * tall, 2 * wide), F32),
+            jax.ShapeDtypeStruct((tall, deep * wide), F32),
+            jax.ShapeDtypeStruct(weights.shape, F32),
+            jax.ShapeDtypeStruct(light.shape, F32),
+        ],
+        in_specs=[hbm] * 2 + [vmem] * 7,
+        scratch_shapes=table(weights, light),
+        compiler_params=SMALL,
+        cost_estimate=pl.CostEstimate(
+            flops=120 * cells, bytes_accessed=8 * cells, transcendentals=8 * cells
+        ),
+        name="inner",
+    )(weights, light, heat, blend, filled.reshape(deep, tall), flat, x_own, z_b, z_a)
     image = pl.pallas_call(
-        brick,
-        out_shape=jax.ShapeDtypeStruct((depth_count, 8, wide), F32),
-        in_specs=[hbm] * 2 + [vmem] * 8,
-        scratch_shapes=[
-            pltpu.VMEM((deep * tall, 2 * wide), F32),
-            pltpu.VMEM((tall, deep * wide), F32),
-            pltpu.SMEM(weights.shape, F32),
-            pltpu.SMEM(light.shape, F32),
-            pltpu.SemaphoreType.DMA((2,)),
-        ],
+        outer,
+        out_shape=shape,
+        in_specs=[vmem] * 11,
+        scratch_shapes=table(weights, light),
         compiler_params=SMALL,
-        name="brick",
-    )(in_hbm(weights), in_hbm(light), heat, blend, filled.reshape(deep, tall), flat, x_own, y_b, z_b, z_a)
+        name="outer",
+    )(near_weights, near_light, heat, blend, flat, y_b, z_b, z_a, part, x_step, veil)
     parts = lax.all_to_all(image, "gz", 0, 0, tiled=True, axis_index_groups=near_groups)
     joined = over(parts.reshape(near, far * 8, wide), near_order, (far * 8, wide))
     parts = lax.all_to_all(

time: 66 us -> 65.4 us (level)
  waiting for transfers between devices: 3.05 us -> 1.49 us
  Pallas kernels: 4.55 us -> 5.25 us
    ppermute x1, waiting for transfers between devices: 3.04 us -> 1.2 us  [on_device(): y_b = lax.ppermute(y_b, 'gy', swap['gy'])]
    pallas_call x1 -> x2, Pallas kernels: 1.76 us -> 2.46 us  [the longest x1 1.54 us: on_device(): pl.pallas_call(inner, out_shape=[shape, jax.ShapeDtypeStruct((deep * tall...]
  transfers between devices with their start and end apart: 4 -> 4, of which waited for: 1 -> 2; matrix products, arithmetic and copies ran while one was open for 0% -> 0% of each run, Pallas kernels for 0% -> 2%
where the time goes in v6:
time: 65.4 us; the launch traced here: 65.1 us
  blocking collectives  44 us (67%)
  starting transfers between devices  14.2 us (22%)
  Pallas kernels  5.25 us (8%)
  waiting for transfers between devices  1.49 us (2%)
    all_to_all x1, blocking collectives, on_device(): lax.all_to_all(joined.reshape(far, 8, wide), 'gz', 0, 0, tiled=True, axis...  33.2 us
    all_to_all x1, blocking collectives, on_device(): lax.all_to_all(image, 'gz', 0, 0, tiled=True, axis_index_groups=near_groups)  10.8 us
    ppermute x1, starting transfers between devices, on_device(): z_a = lax.ppermute(z_a, 'gz', [(i, i ^ 1) for i in range(depth_count)])  6.99 us
    all_to_all x1, starting transfers between devices, on_device(): lax.all_to_all(flat, ('gx', 'gy'), 0, 0, tiled=True, axis_index_groups=se...  4.66 us
    pallas_call x1, Pallas kernels, faces(): pl.pallas_call(face_kernel, out_shape=[jax.ShapeDtypeStruct(s, F32) for s...  2.15 us
    ppermute x1, starting transfers between devices, on_device(): y_b = lax.ppermute(y_b, 'gy', swap['gy'])  1.92 us
    pallas_call x1, Pallas kernels, on_device(): pl.pallas_call(inner, out_shape=[shape, jax.ShapeDtypeStruct((deep * tall...  1.54 us
  transfers between devices with their start and end apart: 4, of which 2 were waited for; matrix products, arithmetic and copies ran while one was open for 0% of the time, Pallas kernels for 2%

profile of v6, /device:TPU:24, one launch (start us, length us, event | category | flops | bytes accessed | tf_op | source)
XLA Modules:
  0.0 65.1 jit_solution(14269885266679728589)
XLA Ops:
  0.0 2.2 %faces.1 = (f32[8,64,128]{2,1,0:T(8,128)S(1)}, f32[8,64,128]{2,1,0:T(8,128)S(1)}, f32[8,2,16,128]{3,2,1,0:T(8,128)}, f32[2,8,128]{2,1,0:T(8,128)S(1)}, f32[2,8,1...) custom-call(f32[8,64,128]{2,1,0:T(8,128)} %far_heat.1, f32[8,64,128]{2,1,0:T(8,128)} %far_blend.1), custom_call_target="tpu_custom_call" | custom-call | tf_op jit(solution)/shard_map/faces/pallas_call | solution.py:89
  2.2 4.7 %all-to-all-start = ((f32[8,2,16,128]{3,2,1,0:T(8,128)}), f32[8,2,16,128]{3,2,1,0:T(8,128)S(1)}, u32[]{:S(2)}, u32[]{:S(2)}) async-start(f32[8,2,16,128]{3,2,1,0:T(8,128)} %get-tuple-element.19), calls=%async_computation | async-start | bytes 262144 | tf_op jit(solution)/shard_map/all_to_all | solution.py:302
  6.8 0.7 %collective-permute-start = (f32[2,64,128]{2,1,0:T(8,128)S(1)}, f32[2,64,128]{2,1,0:T(8,128)S(1)}, u32[]{:S(2)}, u32[]{:S(2)}) collective-permute-start(f32[2,64,128]{2,1,0:T(8,128)S(1)} %get-tuple-element.21), channel_id=1, source_target_pairs={{1,2},{2,1},{3,4},{4,3},{5,6},{6,5},{7,8},{8,7},{9,10},{10,9},{11,... | collective-permute-start | bytes 196616 | tf_op jit(solution)/shard_map/ppermute | solution.py:312
  7.5 7.0 %collective-permute-start.1 = (f32[2,64,128]{2,1,0:T(8,128)S(1)}, f32[2,64,128]{2,1,0:T(8,128)S(1)}, u32[]{:S(2)}, u32[]{:S(2)}) collective-permute-start(f32[2,64,128]{2,1,0:T(8,128)S(1)} %get-tuple-element.22), channel_id=1, source_target_pairs={{0,1},{1,0},{2,3},{3,2},{4,5},{5,4},{6,7},{7,6},{8,9},{9,8},{10,11... | collective-permute-start | bytes 196616 | tf_op jit(solution)/shard_map/ppermute | solution.py:311
  14.5 0.0 copy-start
  14.5 1.9 %collective-permute-start.2 = (f32[2,8,128]{2,1,0:T(8,128)S(1)}, f32[2,8,128]{2,1,0:T(8,128)S(1)}, u32[]{:S(2)}, u32[]{:S(2)}) collective-permute-start(f32[2,8,128]{2,1,0:T(8,128)S(1)} %get-tuple-element.25), channel_id=1, source_target_pairs={{32,64},{64,32},{96,128},{128,96},{160,192},{192,160},{33,65},{65,... | collective-permute-start | bytes 24584 | tf_op jit(solution)/shard_map/ppermute | solution.py:310
  16.4 0.0 collective-permute-done.refs_7_.refs_6_
  16.4 0.3 collective-permute-done.1.refs_8_.refs_7_
  16.7 0.0 all-to-all-done.refs_5_.refs_4_
  16.7 0.0 copy-done
  16.7 1.5 %inner.1 = (f32[32,8,128]{2,1,0:T(8,128)S(1)}, f32[512,256]{1,0:T(8,128)S(1)}, f32[64,1024]{1,0:T(8,128)S(1)}, f32[4,7]{1,0:T(4,128)S(1)}, f32[3]{0:T(128)S(1)}) custom-call(f32[4,7]{1,0:T(4,128)} %refs_0_.1, f32[3]{0:T(128)} %refs_1_.1, f32[8,64,128]{2,1,0:T(8,128)S(1)} %get-tuple-element.17.refs_2_, f32[8,64,128]{2,1,0:T(8,128)S(1)} %get-tuple-element.18.refs_3_, ...), custom_call_target="tpu_custom_call" | custom-call | flops 7864320 | bytes 524288 | tf_op jit(solution)/shard_map/inner/pallas_call | solution.py:334
  18.3 1.2 %collective-permute-done.2.refs_5_ = f32[2,8,128]{2,1,0:T(8,128)S(1)} collective-permute-done((f32[2,8,128]{2,1,0:T(8,128)S(1)}, f32[2,8,128]{2,1,0:T(8,128)S(1)}, u32[]{:S(2)}, u32[]{:S(2)}) %collective-permute-start.2) | collective-permute-done | bytes 8224 | tf_op jit(solution)/shard_map/ppermute | solution.py:310
  19.5 0.9 %outer.1 = f32[32,8,128]{2,1,0:T(8,128)S(1)} custom-call(f32[4,7]{1,0:T(4,128)S(1)} %get-tuple-element.23.refs_0_, f32[3]{0:T(128)S(1)} %get-tuple-element.24.refs_1_, f32[8,64,128]{2,1,0:T(8,128)S(1)} %get-tuple-element.17.refs_2_, f32[8,64,128]{2,1,0:T(8,128)S(1)} %get-tuple-element.18.refs_3_, f32[8,2,16,128]{3,2,1,0:T(8,128)S(1)} %all-to-all-done.refs_5_.refs_4_, ...), custom_call_target="tpu_custom_call" | custom-call | tf_op jit(solution)/shard_map/outer/pallas_call | solution.py:351
  20.4 10.8 %all_to_all.15 = f32[32,8,128]{2,1,0:T(8,128)S(1)} all-to-all(f32[32,8,128]{2,1,0:T(8,128)S(1)} %outer.1), channel_id=1, replica_groups={{2,1,0,3},{6,5,4,7},{10,9,8,11},{14,13,12,15},{18,17,16,19},{22,21,20,2..., dimensions={0} | all-to-all | bytes 262144 | tf_op jit(solution)/shard_map/all_to_all | solution.py:359
  31.2 33.2 %all_to_all.16.refs_0_ = f32[8,8,128]{2,1,0:T(8,128)S(1)} all-to-all(f32[8,8,128]{2,1,0:T(8,128)S(1)} %bitcast.4), channel_id=1, replica_groups={{16,20,24,28,0,4,8,12},{17,21,25,29,1,5,9,13},{18,22,26,30,2,6,10,14},{..., dimensions={0} | all-to-all | bytes 65536 | tf_op jit(solution)/shard_map/all_to_all | solution.py:361
  64.4 0.6 over.3
  (1 shorter events, 0.0 us)
Async XLA Ops:
  2.2 14.5 %all-to-all-start = ((f32[8,2,16,128]{3,2,1,0:T(8,128)}), f32[8,2,16,128]{3,2,1,0:T(8,128)S(1)}, u32[]{:S(2)}, u32[]{:S(2)}) async-start(f32[8,2,16,128]{3,2,1,0:T(8,128)} %get-tuple-element.19), calls=%async_computation | async-start | bytes 262144 | tf_op jit(solution)/shard_map/all_to_all | solution.py:302
  6.8 9.6 %collective-permute-start = (f32[2,64,128]{2,1,0:T(8,128)S(1)}, f32[2,64,128]{2,1,0:T(8,128)S(1)}, u32[]{:S(2)}, u32[]{:S(2)}) collective-permute-start(f32[2,64,128]{2,1,0:T(8,128)S(1)} %get-tuple-element.21), channel_id=1, source_target_pairs={{1,2},{2,1},{3,4},{4,3},{5,6},{6,5},{7,8},{8,7},{9,10},{10,9},{11,... | collective-permute-start | bytes 196616 | tf_op jit(solution)/shard_map/ppermute | solution.py:312
  7.5 9.2 %collective-permute-start.1 = (f32[2,64,128]{2,1,0:T(8,128)S(1)}, f32[2,64,128]{2,1,0:T(8,128)S(1)}, u32[]{:S(2)}, u32[]{:S(2)}) collective-permute-start(f32[2,64,128]{2,1,0:T(8,128)S(1)} %get-tuple-element.22), channel_id=1, source_target_pairs={{0,1},{1,0},{2,3},{3,2},{4,5},{5,4},{6,7},{7,6},{8,9},{9,8},{10,11... | collective-permute-start | bytes 196616 | tf_op jit(solution)/shard_map/ppermute | solution.py:311
  14.5 2.2 %copy-start = (s32[8,64,1]{1,2,0:T(1,128)S(1)}, s32[8,64,1]{1,2,0:T(1,128)}, u32[]{:S(2)}) copy-start(s32[8,64,1]{1,2,0:T(1,128)} %param.7) | copy-start | bytes 6148
  14.5 5.0 %collective-permute-start.2 = (f32[2,8,128]{2,1,0:T(8,128)S(1)}, f32[2,8,128]{2,1,0:T(8,128)S(1)}, u32[]{:S(2)}, u32[]{:S(2)}) collective-permute-start(f32[2,8,128]{2,1,0:T(8,128)S(1)} %get-tuple-element.25), channel_id=1, source_target_pairs={{32,64},{64,32},{96,128},{128,96},{160,192},{192,160},{33,65},{65,... | collective-permute-start | bytes 24584 | tf_op jit(solution)/shard_map/ppermute | solution.py:310

commit v7 on v6

--- a/solution.py
+++ b/solution.py
@@ -61,6 +61,7 @@
             for side in range(2):
                 at = 2 * f + side
                 x_faces[side, f, part : part + 1, :] = turned[at : at + 1]
+    flat[:, 2] = jnp.zeros((flat.shape[0], deep, wide), F32)
     column, columns = lax.axis_index("gx"), lax.axis_size("gx")
     core = lax.axis_index("gy") % 2
     for f, field in enumerate((heat, blend)):
@@ -72,19 +73,19 @@
         y_b[f] = jnp.where(odd_y, high, low)
         beside = jnp.where(odd_y, low, high)
         left, right = x_faces[0, f], x_faces[1, f]
-        x_own[f] = jnp.where(column == 0, left, right)
+        x_own[0, f] = left
+        x_own[1, f] = right
         for i in range(columns):
             other = (i + 1) % columns
             along = jnp.where(column < other, right, left)
             for place, its in ((2 * i, 1), (2 * i + 1, 0)):
-                flat[place, f, 0:deep, :] = jnp.where(core == its, along, beside)
-                flat[place, f, deep:, :] = jnp.zeros((deep, wide), F32)
+                flat[place, f] = jnp.where(core == its, along, beside)
 
 
 def faces(heat, blend):
     deep, tall, wide = heat.shape
     members = 2 * lax.axis_size("gx")
-    shapes = [heat.shape] * 2 + [(members, 2, 2 * deep, wide)] + [(2, deep, wide)] * 2
+    shapes = [heat.shape] * 2 + [(members, 3, deep, wide), (2, 2, deep, wide), (2, deep, wide)]
     shapes += [(2, tall, wide)] * 2
     return pl.pallas_call(
         face_kernel,
@@ -140,9 +141,9 @@
     right = seat(lax.rem(column + 1, columns), core, columns)
     parts = deep * tall // wide
     sides = []
-    for edge, place in ((first, left), (last, right)):
+    for side, edge, place in ((0, first, left), (1, last, right)):
         for f in range(2):
-            face = jnp.where(edge, x_own[f], flat[place, f, 0:deep, :])
+            face = jnp.where(edge, x_own[side, f], flat[place, f]) - x_own[1 - side, f]
             sides.append(jnp.concatenate([face[p : p + 1] for p in range(parts)], axis=1))
     sides = jnp.concatenate(sides + [jnp.zeros((4, deep * tall), F32)], axis=0)
     sides = jnp.concatenate(split3(sides) + [jnp.zeros_like(sides)], axis=0).astype(jnp.bfloat16)
@@ -193,9 +194,6 @@
     base = [w[r][6] + w[r][2] + w[r][3] for r in range(4)]
     sun = [light[i] * 0.5 for i in range(3)]
     fields = (heat, blend)
-    lane8 = lax.broadcasted_iota(jnp.int32, (8, wide), 1)
-    not_first = lane8 > 0
-    not_last = lane8 < wide - 1
     for block in blocks:
         top = 8 * block
         rows = slice(top, top + 8)
@@ -230,8 +228,8 @@
                 else:
                     down = field[z, top + 1 : top + 9, :]
                 dy = down - up
-                right = jnp.where(not_last, pltpu.roll(here, wide - 1, 1), 0.0)
-                left = jnp.where(not_first, pltpu.roll(here, 1, 1), 0.0)
+                right = pltpu.roll(here, wide - 1, 1)
+                left = pltpu.roll(here, 1, 1)
                 outer = x_step[z * tall + top : z * tall + top + 8, index * wide : (index + 1) * wide]
                 dx = right - left + outer
                 slopes.append((here, dz, dy, dx))

time: 65.4 us -> 65.4 us (level)
  no operation moved by 1% of the time
where the time goes in v7:
time: 65.4 us; the launch traced here: 65 us
  blocking collectives  44 us (67%)
  starting transfers between devices  14.2 us (22%)
  Pallas kernels  5.2 us (8%)
  waiting for transfers between devices  1.51 us (2%)
    all_to_all x1, blocking collectives, on_device(): lax.all_to_all(joined.reshape(far, 8, wide), 'gz', 0, 0, tiled=True, axis...  33.2 us
    all_to_all x1, blocking collectives, on_device(): lax.all_to_all(image, 'gz', 0, 0, tiled=True, axis_index_groups=near_groups)  10.8 us
    ppermute x1, starting transfers between devices, on_device(): z_a = lax.ppermute(z_a, 'gz', [(i, i ^ 1) for i in range(depth_count)])  6.99 us
    all_to_all x1, starting transfers between devices, on_device(): lax.all_to_all(flat, ('gx', 'gy'), 0, 0, tiled=True, axis_index_groups=se...  4.66 us
    pallas_call x1, Pallas kernels, faces(): pl.pallas_call(face_kernel, out_shape=[jax.ShapeDtypeStruct(s, F32) for s...  2.13 us
    ppermute x1, starting transfers between devices, on_device(): y_b = lax.ppermute(y_b, 'gy', swap['gy'])  1.92 us
    pallas_call x1, Pallas kernels, on_device(): pl.pallas_call(inner, out_shape=[shape, jax.ShapeDtypeStruct((deep * tall...  1.51 us
  transfers between devices with their start and end apart: 4, of which 2 were waited for; matrix products, arithmetic and copies ran while one was open for 0% of the time, Pallas kernels for 2%

profile of v7, /device:TPU:24, one launch (start us, length us, event | category | flops | bytes accessed | tf_op | source)
XLA Modules:
  0.0 65.0 jit_solution(14913926163038692964)
XLA Ops:
  0.0 2.1 %faces.1 = (f32[8,64,128]{2,1,0:T(8,128)S(1)}, f32[8,64,128]{2,1,0:T(8,128)S(1)}, f32[8,3,8,128]{3,2,1,0:T(8,128)}, f32[2,2,8,128]{3,2,1,0:T(8,128)S(1)}, f32[2,...) custom-call(f32[8,64,128]{2,1,0:T(8,128)} %far_heat.1, f32[8,64,128]{2,1,0:T(8,128)} %far_blend.1), custom_call_target="tpu_custom_call" | custom-call | tf_op jit(solution)/shard_map/faces/pallas_call | solution.py:90
  2.1 4.7 %all-to-all-start = ((f32[8,3,8,128]{3,2,1,0:T(8,128)}), f32[8,3,8,128]{3,2,1,0:T(8,128)S(1)}, u32[]{:S(2)}, u32[]{:S(2)}) async-start(f32[8,3,8,128]{3,2,1,0:T(8,128)} %get-tuple-element.19), calls=%async_computation | async-start | bytes 196608 | tf_op jit(solution)/shard_map/all_to_all | solution.py:300
  6.8 0.7 %collective-permute-start = (f32[2,64,128]{2,1,0:T(8,128)S(1)}, f32[2,64,128]{2,1,0:T(8,128)S(1)}, u32[]{:S(2)}, u32[]{:S(2)}) collective-permute-start(f32[2,64,128]{2,1,0:T(8,128)S(1)} %get-tuple-element.21), channel_id=1, source_target_pairs={{1,2},{2,1},{3,4},{4,3},{5,6},{6,5},{7,8},{8,7},{9,10},{10,9},{11,... | collective-permute-start | bytes 196616 | tf_op jit(solution)/shard_map/ppermute | solution.py:310
  7.5 7.0 %collective-permute-start.1 = (f32[2,64,128]{2,1,0:T(8,128)S(1)}, f32[2,64,128]{2,1,0:T(8,128)S(1)}, u32[]{:S(2)}, u32[]{:S(2)}) collective-permute-start(f32[2,64,128]{2,1,0:T(8,128)S(1)} %get-tuple-element.22), channel_id=1, source_target_pairs={{0,1},{1,0},{2,3},{3,2},{4,5},{5,4},{6,7},{7,6},{8,9},{9,8},{10,11... | collective-permute-start | bytes 196616 | tf_op jit(solution)/shard_map/ppermute | solution.py:309
  14.5 0.0 copy-start
  14.5 1.9 %collective-permute-start.2 = (f32[2,8,128]{2,1,0:T(8,128)S(1)}, f32[2,8,128]{2,1,0:T(8,128)S(1)}, u32[]{:S(2)}, u32[]{:S(2)}) collective-permute-start(f32[2,8,128]{2,1,0:T(8,128)S(1)} %get-tuple-element.25), channel_id=1, source_target_pairs={{32,64},{64,32},{96,128},{128,96},{160,192},{192,160},{33,65},{65,... | collective-permute-start | bytes 24584 | tf_op jit(solution)/shard_map/ppermute | solution.py:308
  16.4 0.0 collective-permute-done.refs_7_.refs_6_
  16.4 0.3 collective-permute-done.1.refs_8_.refs_7_
  16.7 0.0 all-to-all-done.refs_5_.refs_4_
  16.7 0.0 copy-done
  16.7 1.5 %inner.1 = (f32[32,8,128]{2,1,0:T(8,128)S(1)}, f32[512,256]{1,0:T(8,128)S(1)}, f32[64,1024]{1,0:T(8,128)S(1)}, f32[4,7]{1,0:T(4,128)S(1)}, f32[3]{0:T(128)S(1)}) custom-call(f32[4,7]{1,0:T(4,128)} %refs_0_.1, f32[3]{0:T(128)} %refs_1_.1, f32[8,64,128]{2,1,0:T(8,128)S(1)} %get-tuple-element.17.refs_2_, f32[8,64,128]{2,1,0:T(8,128)S(1)} %get-tuple-element.18.refs_3_, ...), custom_call_target="tpu_custom_call" | custom-call | flops 7864320 | bytes 524288 | tf_op jit(solution)/shard_map/inner/pallas_call | solution.py:332
  18.2 1.2 %collective-permute-done.2.refs_5_ = f32[2,8,128]{2,1,0:T(8,128)S(1)} collective-permute-done((f32[2,8,128]{2,1,0:T(8,128)S(1)}, f32[2,8,128]{2,1,0:T(8,128)S(1)}, u32[]{:S(2)}, u32[]{:S(2)}) %collective-permute-start.2) | collective-permute-done | bytes 8224 | tf_op jit(solution)/shard_map/ppermute | solution.py:308
  19.4 0.9 %outer.1 = f32[32,8,128]{2,1,0:T(8,128)S(1)} custom-call(f32[4,7]{1,0:T(4,128)S(1)} %get-tuple-element.23.refs_0_, f32[3]{0:T(128)S(1)} %get-tuple-element.24.refs_1_, f32[8,64,128]{2,1,0:T(8,128)S(1)} %get-tuple-element.17.refs_2_, f32[8,64,128]{2,1,0:T(8,128)S(1)} %get-tuple-element.18.refs_3_, f32[8,3,8,128]{3,2,1,0:T(8,128)S(1)} %all-to-all-done.refs_5_.refs_4_, ...), custom_call_target="tpu_custom_call" | custom-call | tf_op jit(solution)/shard_map/outer/pallas_call | solution.py:349
  20.4 10.8 %all_to_all.15 = f32[32,8,128]{2,1,0:T(8,128)S(1)} all-to-all(f32[32,8,128]{2,1,0:T(8,128)S(1)} %outer.1), channel_id=1, replica_groups={{2,1,0,3},{6,5,4,7},{10,9,8,11},{14,13,12,15},{18,17,16,19},{22,21,20,2..., dimensions={0} | all-to-all | bytes 262144 | tf_op jit(solution)/shard_map/all_to_all | solution.py:357
  31.2 33.2 %all_to_all.16.refs_0_ = f32[8,8,128]{2,1,0:T(8,128)S(1)} all-to-all(f32[8,8,128]{2,1,0:T(8,128)S(1)} %bitcast.4), channel_id=1, replica_groups={{16,20,24,28,0,4,8,12},{17,21,25,29,1,5,9,13},{18,22,26,30,2,6,10,14},{..., dimensions={0} | all-to-all | bytes 65536 | tf_op jit(solution)/shard_map/all_to_all | solution.py:359
  64.4 0.6 over.3
  (1 shorter events, 0.0 us)
Async XLA Ops:
  2.1 14.5 %all-to-all-start = ((f32[8,3,8,128]{3,2,1,0:T(8,128)}), f32[8,3,8,128]{3,2,1,0:T(8,128)S(1)}, u32[]{:S(2)}, u32[]{:S(2)}) async-start(f32[8,3,8,128]{3,2,1,0:T(8,128)} %get-tuple-element.19), calls=%async_computation | async-start | bytes 196608 | tf_op jit(solution)/shard_map/all_to_all | solution.py:300
  6.8 9.6 %collective-permute-start = (f32[2,64,128]{2,1,0:T(8,128)S(1)}, f32[2,64,128]{2,1,0:T(8,128)S(1)}, u32[]{:S(2)}, u32[]{:S(2)}) collective-permute-start(f32[2,64,128]{2,1,0:T(8,128)S(1)} %get-tuple-element.21), channel_id=1, source_target_pairs={{1,2},{2,1},{3,4},{4,3},{5,6},{6,5},{7,8},{8,7},{9,10},{10,9},{11,... | collective-permute-start | bytes 196616 | tf_op jit(solution)/shard_map/ppermute | solution.py:310
  7.5 9.2 %collective-permute-start.1 = (f32[2,64,128]{2,1,0:T(8,128)S(1)}, f32[2,64,128]{2,1,0:T(8,128)S(1)}, u32[]{:S(2)}, u32[]{:S(2)}) collective-permute-start(f32[2,64,128]{2,1,0:T(8,128)S(1)} %get-tuple-element.22), channel_id=1, source_target_pairs={{0,1},{1,0},{2,3},{3,2},{4,5},{5,4},{6,7},{7,6},{8,9},{9,8},{10,11... | collective-permute-start | bytes 196616 | tf_op jit(solution)/shard_map/ppermute | solution.py:309
  14.5 2.2 %copy-start = (s32[8,64,1]{1,2,0:T(1,128)S(1)}, s32[8,64,1]{1,2,0:T(1,128)}, u32[]{:S(2)}) copy-start(s32[8,64,1]{1,2,0:T(1,128)} %param.7) | copy-start | bytes 6148
  14.5 5.0 %collective-permute-start.2 = (f32[2,8,128]{2,1,0:T(8,128)S(1)}, f32[2,8,128]{2,1,0:T(8,128)S(1)}, u32[]{:S(2)}, u32[]{:S(2)}) collective-permute-start(f32[2,8,128]{2,1,0:T(8,128)S(1)} %get-tuple-element.25), channel_id=1, source_target_pairs={{32,64},{64,32},{96,128},{128,96},{160,192},{192,160},{33,65},{65,... | collective-permute-start | bytes 24584 | tf_op jit(solution)/shard_map/ppermute | solution.py:308
